TPU v7x, 32 devices: a whole 2x2x4 slice. The times are simulated.
32 devices in a mesh: dp: 8 (over z, y), tensor: 4 (over x, core).
Axes of the slice: x: 2, y: 2, z: 4, core: 2. Of those that a mesh axis runs over, the one named last changes fastest.
Arguments:
- block_input: bfloat16 [4, 8192, 512], P(None, 'dp'), may hold values from -6 to 6
- cotangent: bfloat16 [4, 8192, 512], P(None, 'dp'), may hold values from -6 to 6
- source: int32 [4, 8192], replicated, may hold values from 0 to 8191, as said below
- seq_lengths: int32 [4, 8, 3], P(None, 'dp'), may hold values from 1 to 682, 1024 in all within a row
- qkv_weight: bfloat16 [3, 512, 512], P(None, None, 'tensor'), may hold values from -0.375 to 0.375
- qv_bias: bfloat16 [2, 512], P(None, 'tensor'), may hold values from -3 to 3
- out_weight: bfloat16 [512, 512], P('tensor'), may hold values from -0.75 to 0.75
- out_bias: bfloat16 [512], replicated, may hold values from -3 to 3
- up_weight: bfloat16 [512, 2048], P(None, 'tensor'), may hold values from -0.25 to 0.25
- up_bias: bfloat16 [2048], P('tensor'), may hold values from -3 to 3
- down_weight: bfloat16 [2048, 512], P('tensor'), may hold values from -0.25 to 0.25
- down_bias: bfloat16 [512], replicated, may hold values from -3 to 3
- rezero_alphas: float32 [2], replicated, may hold values from 0.2 to 0.45
Outputs:
- layer_output: float32 [4, 8192, 512], P(None, 'dp')
- input_grad: float32 [4, 8192, 512], P(None, 'dp')
- qkv_weight_grad: float32 [3, 512, 512], P(None, None, 'tensor')
- qv_bias_grad: float32 [2, 512], P(None, 'tensor')
- out_weight_grad: float32 [512, 512], P('tensor')
- out_bias_grad: float32 [512], replicated
- up_weight_grad: float32 [512, 2048], P(None, 'tensor')
- up_bias_grad: float32 [2048], P('tensor')
- down_weight_grad: float32 [2048, 512], P('tensor')
- down_bias_grad: float32 [512], replicated
- alphas_grad: float32 [2], replicated
Inputs may be any that keep to these rules, and one draw needn't show every extreme that they name: In each micro-batch source is a permutation of the input rows; the 1024 rows of one device go to every group in equal numbers, 128 each. `seq_lengths`: each row of 3 lengths sums to 1024.
All inputs are finite; a program needn't handle non-finite values.
Results may differ from a plain program's by a relative error of at most 0.011.
The roundings to bfloat16 on the way count: a program that leaves them out, or rounds other values in their place, can miss the bound.
Values may be sent and summed in bfloat16 or wider, within the bound.
No kernel may reach another device: no remote copies, remote signals or barrier semaphores. Data moves between devices by JAX's collectives and lax.ppermute only.
A program may use at most 256 MiB of HBM per device.

v0:
```python
import jax
import jax.numpy as jnp
from jax import lax
from jax.sharding import PartitionSpec as P

HEAD_SIZE = 64
SEQS = 3
BLK = 128
QBLK = 512
TOK_GRP = 1024
SLOTS = 1536


def layouts(lengths_row):
    numbers = jnp.arange(SEQS, dtype=jnp.int32)
    earlier = numbers[None, :] < numbers[:, None]
    padded = (lengths_row + BLK - 1) // BLK * BLK
    real_start = jnp.sum(jnp.where(earlier, lengths_row[None, :], 0), axis=1, dtype=jnp.int32)
    slot_start = jnp.sum(jnp.where(earlier, padded[None, :], 0), axis=1, dtype=jnp.int32)
    ranks = jnp.arange(TOK_GRP, dtype=jnp.int32)
    inside = (ranks[:, None] >= real_start[None, :]) & (
        ranks[:, None] < (real_start + lengths_row)[None, :]
    )
    slot_of_rank = ranks + jnp.sum(
        jnp.where(inside, (slot_start - real_start)[None, :], 0), axis=1, dtype=jnp.int32
    )
    cells = jnp.arange(SLOTS, dtype=jnp.int32)
    within = (cells[:, None] >= slot_start[None, :]) & (
        cells[:, None] < (slot_start + lengths_row)[None, :]
    )
    segment = jnp.sum(jnp.where(within, numbers[None, :] + 1, 0), axis=1, dtype=jnp.int32) - 1
    rank_of_slot = (
        jnp.sum(
            jnp.where(within, cells[:, None] - slot_start[None, :] + real_start[None, :] + 1, 0),
            axis=1,
            dtype=jnp.int32,
        )
        - 1
    )
    return (slot_of_rank, rank_of_slot, segment)


def masked_scores(query_block, key_heads, segment, first_row, score_scale):
    rows_here = first_row + jnp.arange(QBLK, dtype=jnp.int32)
    columns = jnp.arange(SLOTS, dtype=jnp.int32)
    segment_rows = lax.dynamic_slice_in_dim(segment, first_row, QBLK)
    allowed = (segment_rows[:, None] == segment[None, :]) & (segment_rows[:, None] >= 0) & (
        columns[None, :] <= rows_here[:, None]
    ) | (columns[None, :] == rows_here[:, None])
    raw_scores = jnp.einsum(
        "qhe,khe->hqk", query_block, key_heads, preferred_element_type=jnp.float32
    )
    return jnp.where(allowed[None, :, :], raw_scores * score_scale, -1e30)


def gelu_tanh(value):
    return jax.nn.gelu(value, approximate=True)


def per_device(
    block_input,
    cotangent,
    source,
    seq_lengths,
    qkv_weight,
    qv_bias,
    out_weight,
    out_bias,
    up_weight,
    up_bias,
    down_weight,
    down_bias,
    rezero_alphas,
):
    micro_count, tok_rows, model_width = block_input.shape
    group_id = lax.axis_index("dp")
    tensor_id = lax.axis_index("tensor")
    tensor_count = lax.axis_size("tensor")
    own_rows = SLOTS // tensor_count
    own_start = tensor_id * own_rows
    local_width = qkv_weight.shape[2]
    local_heads = local_width // HEAD_SIZE
    score_scale = HEAD_SIZE ** (-0.5)
    alpha_first = rezero_alphas[0]
    alpha_second = rezero_alphas[1]
    block_starts = jnp.arange(SLOTS // QBLK, dtype=jnp.int32) * QBLK
    qkv_grad_sum = jnp.zeros(qkv_weight.shape, jnp.float32)
    qv_bias_sum = jnp.zeros(qv_bias.shape, jnp.float32)
    out_grad_sum = jnp.zeros(out_weight.shape, jnp.float32)
    small_sum = jnp.zeros((2 + 2 * model_width,), jnp.float32)
    up_grad_sum = jnp.zeros(up_weight.shape, jnp.float32)
    down_grad_sum = jnp.zeros(down_weight.shape, jnp.float32)
    up_bias_sum = jnp.zeros(up_bias.shape, jnp.float32)
    output_list = []
    grad_list = []
    for micro_index in range(micro_count):
        positions = source[micro_index]
        owners = positions // tok_rows
        mine_slots = jnp.nonzero(owners == group_id, size=tok_rows)[0].astype(jnp.int32)
        send_rows = positions[mine_slots] - group_id * tok_rows
        arrived_input, arrived_grad = (
            lax.all_to_all(
                block_input[micro_index][send_rows], "dp", split_axis=0, concat_axis=0, tiled=True
            ),
            lax.all_to_all(
                cotangent[micro_index][send_rows], "dp", split_axis=0, concat_axis=0, tiled=True
            ),
        )
        group_block = lax.dynamic_slice_in_dim(positions, group_id * tok_rows, tok_rows)
        arrival_rank = jnp.argsort(group_block // tok_rows, stable=True)
        row_of_rank = (
            jnp.zeros((tok_rows,), jnp.int32)
            .at[arrival_rank]
            .set(jnp.arange(tok_rows, dtype=jnp.int32))
        )
        slot_of_rank, rank_of_slot, segment = layouts(seq_lengths[micro_index, 0])
        own_ranks = lax.dynamic_slice_in_dim(rank_of_slot, own_start, own_rows)
        filled = own_ranks >= 0
        chosen = row_of_rank[jnp.maximum(own_ranks, 0)]
        input_own = jnp.where(filled[:, None], arrived_input[chosen], jnp.zeros((), jnp.bfloat16))
        grad_own = jnp.where(filled[:, None], arrived_grad[chosen].astype(jnp.float32), 0.0)
        gathered = lax.all_gather(input_own, "tensor", axis=0, tiled=True)
        projected = jnp.einsum(
            "sd,cde->cse", gathered, qkv_weight, preferred_element_type=jnp.float32
        )
        queries = (
            (projected[0] + qv_bias[0]).astype(jnp.bfloat16).reshape(SLOTS, local_heads, HEAD_SIZE)
        )
        keys_all = projected[1].astype(jnp.bfloat16).reshape(SLOTS, local_heads, HEAD_SIZE)
        values_all = (
            (projected[2] + qv_bias[1]).astype(jnp.bfloat16).reshape(SLOTS, local_heads, HEAD_SIZE)
        )

        def forward_block(first_row):
            query_block = lax.dynamic_slice_in_dim(queries, first_row, QBLK)
            scores = masked_scores(query_block, keys_all, segment, first_row, score_scale)
            row_top = jnp.max(scores, axis=-1, keepdims=True)
            shifted = jnp.exp(scores - row_top)
            row_total = jnp.sum(shifted, axis=-1, keepdims=True)
            weights = (shifted / row_total).astype(jnp.bfloat16)
            mixed_block = jnp.einsum(
                "hqk,khe->qhe", weights, values_all, preferred_element_type=jnp.float32
            )
            return (mixed_block.astype(jnp.bfloat16), (row_top + jnp.log(row_total))[:, :, 0])

        mixed_blocks, log_totals = lax.map(forward_block, block_starts)
        mixed = mixed_blocks.reshape(SLOTS, local_width)
        attn_own = (
            lax.psum_scatter(
                jnp.dot(mixed, out_weight, preferred_element_type=jnp.float32),
                "tensor",
                scatter_dimension=0,
                tiled=True,
            )
            + out_bias
        )
        hidden_own = input_own.astype(jnp.float32) + alpha_first * attn_own
        hidden_low = hidden_own.astype(jnp.bfloat16)
        grad_branch = None
        hidden_all = lax.all_gather(hidden_low, "tensor", axis=0, tiled=True)
        pre_act = jnp.dot(hidden_all, up_weight, preferred_element_type=jnp.float32) + up_bias
        act_value, gelu_pull = jax.vjp(gelu_tanh, pre_act)
        activated = act_value.astype(jnp.bfloat16)
        branch_own = (
            lax.psum_scatter(
                jnp.dot(
                    lax.slice_in_dim(activated, 0, own_rows * lax.axis_size("tensor"), axis=0),
                    down_weight,
                    preferred_element_type=jnp.float32,
                ),
                "tensor",
                scatter_dimension=0,
                tiled=True,
            )
            + down_bias
        )
        output_own = hidden_own + alpha_second * branch_own
        grad_branch = (alpha_second * grad_own).astype(jnp.bfloat16)
        branch_all = lax.all_gather(grad_branch, "tensor", axis=0, tiled=True)
        down_grad_sum = down_grad_sum + jnp.einsum(
            "sf,sd->fd", activated, branch_all, preferred_element_type=jnp.float32
        )
        grad_act = jnp.einsum(
            "sd,fd->sf", branch_all, down_weight, preferred_element_type=jnp.float32
        )
        grad_pre = gelu_pull(grad_act)[0].astype(jnp.bfloat16)
        up_bias_sum = up_bias_sum + jnp.sum(grad_pre.astype(jnp.float32), axis=0)
        up_grad_sum = up_grad_sum + jnp.einsum(
            "sd,sf->df", hidden_all, grad_pre, preferred_element_type=jnp.float32
        )
        grad_hidden = grad_own + lax.psum_scatter(
            jnp.einsum(
                "sf,df->sd",
                lax.slice_in_dim(grad_pre, 0, own_rows * lax.axis_size("tensor"), axis=0),
                up_weight,
                preferred_element_type=jnp.float32,
            ),
            "tensor",
            scatter_dimension=0,
            tiled=True,
        )
        alpha_two = jnp.sum(grad_own * branch_own)
        down_bias_part = jnp.sum(grad_branch.astype(jnp.float32), axis=0)
        grad_attn = (alpha_first * grad_hidden).astype(jnp.bfloat16)
        alpha_one = jnp.sum(grad_hidden * attn_own)
        out_bias_part = jnp.sum(grad_attn.astype(jnp.float32), axis=0)
        attn_all = lax.all_gather(grad_attn, "tensor", axis=0, tiled=True)
        out_grad_sum = out_grad_sum + jnp.einsum(
            "sh,sd->hd", mixed, attn_all, preferred_element_type=jnp.float32
        )
        grad_mixed = jnp.einsum(
            "sd,hd->sh", attn_all, out_weight, preferred_element_type=jnp.float32
        ).astype(jnp.bfloat16)
        grad_heads = grad_mixed.reshape(SLOTS, local_heads, HEAD_SIZE)

        def backward_block(carry, first_row):
            key_total, value_total = carry
            query_block = lax.dynamic_slice_in_dim(queries, first_row, QBLK)
            grad_block = lax.dynamic_slice_in_dim(grad_heads, first_row, QBLK)
            log_block = lax.dynamic_index_in_dim(log_totals, first_row // QBLK, 0, keepdims=False)
            scores = masked_scores(query_block, keys_all, segment, first_row, score_scale)
            weights = jnp.exp(scores - log_block[:, :, None])
            low_weights = weights.astype(jnp.bfloat16)
            grad_weights = jnp.einsum(
                "qhe,khe->hqk", grad_block, values_all, preferred_element_type=jnp.float32
            )
            inner_total = jnp.sum(weights * grad_weights, axis=-1, keepdims=True)
            grad_scores = (score_scale * weights * (grad_weights - inner_total)).astype(
                jnp.bfloat16
            )
            grad_query = jnp.einsum(
                "hqk,khe->qhe", grad_scores, keys_all, preferred_element_type=jnp.float32
            )
            key_total = key_total + jnp.einsum(
                "hqk,qhe->khe", grad_scores, query_block, preferred_element_type=jnp.float32
            )
            value_total = value_total + jnp.einsum(
                "hqk,qhe->khe", low_weights, grad_block, preferred_element_type=jnp.float32
            )
            return ((key_total, value_total), grad_query.astype(jnp.bfloat16))

        start_carry = (
            jnp.zeros((SLOTS, local_heads, HEAD_SIZE), jnp.float32),
            jnp.zeros((SLOTS, local_heads, HEAD_SIZE), jnp.float32),
        )
        (key_total, value_total), grad_query = lax.scan(backward_block, start_carry, block_starts)
        grad_q = grad_query.reshape(SLOTS, local_width)
        grad_k = key_total.astype(jnp.bfloat16).reshape(SLOTS, local_width)
        grad_v = value_total.astype(jnp.bfloat16).reshape(SLOTS, local_width)
        grad_qkv = jnp.stack([grad_q, grad_k, grad_v])
        qv_bias_sum = qv_bias_sum + jnp.stack(
            [
                jnp.sum(grad_q.astype(jnp.float32), axis=0),
                jnp.sum(grad_v.astype(jnp.float32), axis=0),
            ]
        )
        qkv_grad_sum = qkv_grad_sum + jnp.einsum(
            "sd,cse->cde", gathered, grad_qkv, preferred_element_type=jnp.float32
        )
        grad_input_own = grad_hidden + lax.psum_scatter(
            jnp.einsum("cse,cde->sd", grad_qkv, qkv_weight, preferred_element_type=jnp.float32),
            "tensor",
            scatter_dimension=0,
            tiled=True,
        )
        small_terms = jnp.concatenate(
            [jnp.stack([alpha_one, alpha_two]), out_bias_part, down_bias_part]
        )
        arrival_slots = slot_of_rank[arrival_rank]
        output_all, grad_input_all, small_all = (
            lax.all_gather(output_own, "tensor", axis=0, tiled=True),
            lax.all_gather(grad_input_own, "tensor", axis=0, tiled=True),
            lax.all_gather(small_terms[None, :], "tensor", axis=0, tiled=True),
        )
        small_sum = small_sum + jnp.sum(small_all, axis=0)
        returned_output, returned_grad = (
            lax.all_to_all(
                output_all[arrival_slots], "dp", split_axis=0, concat_axis=0, tiled=True
            ),
            lax.all_to_all(
                grad_input_all[arrival_slots], "dp", split_axis=0, concat_axis=0, tiled=True
            ),
        )
        output_list.append(
            jnp.zeros((tok_rows, model_width), jnp.float32).at[send_rows].set(returned_output)
        )
        grad_list.append(
            jnp.zeros((tok_rows, model_width), jnp.float32).at[send_rows].set(returned_grad)
        )
    totals = lax.psum(
        (
            qkv_grad_sum,
            qv_bias_sum,
            out_grad_sum,
            up_grad_sum,
            up_bias_sum,
            down_grad_sum,
            small_sum,
        ),
        "dp",
    )
    small_total = totals[6]
    layer_output = jnp.stack(output_list)
    input_grad = jnp.stack(grad_list)
    return (
        layer_output,
        input_grad,
        totals[0],
        totals[1],
        totals[2],
        small_total[2 : 2 + model_width],
        totals[3],
        totals[4],
        totals[5],
        small_total[2 + model_width :],
        small_total[0:2],
    )


def solution(mesh):
    in_specs = (
        P(None, "dp", None),
        P(None, "dp", None),
        P(),
        P(None, "dp", None),
        P(None, None, "tensor"),
        P(None, "tensor"),
        P("tensor", None),
        P(),
        P(None, "tensor"),
        P("tensor"),
        P("tensor", None),
        P(),
        P(),
    )
    out_specs = (
        P(None, "dp", None),
        P(None, "dp", None),
        P(None, None, "tensor"),
        P(None, "tensor"),
        P("tensor", None),
        P(),
        P(None, "tensor"),
        P("tensor"),
        P("tensor", None),
        P(),
        P(),
    )
    return jax.shard_map(
        per_device, mesh=mesh, in_specs=in_specs, out_specs=out_specs, check_vma=False
    )
```

profile of v0, /device:TPU:0, one launch (start us, length us, event | category | flops | bytes accessed | tf_op | source)
XLA Modules:
  0.0 1957.9 jit_solution(16758753535124627800)
XLA Ops:
  9.3 57.0 %scatter_custom_fusion.6 = s32[1024]{0:T(1024)S(1)} fusion(s32[8192]{0:T(1024)S(1)} %bitcast.638, s32[8192]{0:T(1024)S(1)} %ne.322, s32[]{:T(128)} %constant.574.clone.1), kind=kCustom, calls=%fused_computation.674 | custom fusion | flops 8192 | bytes 4100 | tf_op jit(solution)/shard_map/scatter-add | solution.py:99
  98.9 56.9 %scatter_custom_fusion.9 = s32[1024]{0:T(1024)S(1)} fusion(s32[8192]{0:T(1024)S(1)} %bitcast.640, s32[8192]{0:T(1024)S(1)} %ne.322, s32[]{:T(128)} %constant.574.clone.1), kind=kCustom, calls=%fused_computation.670 | custom fusion | flops 8192 | bytes 4100 | tf_op jit(solution)/shard_map/scatter-add | solution.py:99
  167.6 57.0 %scatter_custom_fusion.3 = s32[1024]{0:T(1024)S(1)} fusion(s32[8192]{0:T(1024)S(1)} %bitcast.637, s32[8192]{0:T(1024)S(1)} %ne.322, s32[]{:T(128)} %constant.574.clone.1), kind=kCustom, calls=%fused_computation.678 | custom fusion | flops 8192 | bytes 4100 | tf_op jit(solution)/shard_map/scatter-add | solution.py:99
  283.7 57.0 %scatter_custom_fusion = s32[1024]{0:T(1024)S(1)} fusion(s32[8192]{0:T(1024)S(1)} %bitcast.639, s32[8192]{0:T(1024)S(1)} %ne.322, s32[]{:T(128)} %constant.574.clone.1), kind=kCustom, calls=%fused_computation.684 | custom fusion | flops 8192 | bytes 4100 | tf_op jit(solution)/shard_map/scatter-add | solution.py:99
  427.6 33.3 %while.117 = (s32[]{:T(128)}, bf16[3,512,2,64]{1,3,2,0:T(8,128)(2,1)}, f32[3,2,512]{2,1,0:T(2,128)S(1)}, s32[3]{0:T(128)S(1)}, s32[1536]{0:T(1024)S(1)}, /*index...) while((s32[]{:T(128)}, ...), condition=%wide.region_35.36_spmd, body=%wide.region_32.35_spmd.sunk | while | flops 426311680 | bytes 23119032 | solution.py:146
  466.1 34.3 %while.118 = (s32[]{:T(128)}, bf16[3,512,2,64]{1,3,2,0:T(8,128)(2,1)S(1)}, f32[3,2,512]{2,1,0:T(2,128)S(1)}, s32[3]{0:T(128)S(1)}, s32[1536]{0:T(1024)S(1)}, /*i...) while((s32[]{:T(128)}, ...), condition=%wide.region_55.56_spmd, body=%wide.region_52.55_spmd.sunk | while | flops 426311680 | bytes 23119032 | solution.py:146
  503.6 34.3 %while.119 = (s32[]{:T(128)}, bf16[3,512,2,64]{1,3,2,0:T(8,128)(2,1)S(1)}, f32[3,2,512]{2,1,0:T(2,128)S(1)}, s32[3]{0:T(128)S(1)}, s32[1536]{0:T(1024)S(1)}, /*i...) while((s32[]{:T(128)}, ...), condition=%wide.region_75.76_spmd, body=%wide.region_72.75_spmd.sunk | while | flops 426311680 | bytes 23119032 | solution.py:146
  557.8 25.4 %all-to-all-done.12 = bf16[8,128,512]{2,1,0:T(8,128)(2,1)} async-done(((bf16[8,128,512]{2,1,0:T(8,128)(2,1)}), bf16[8,128,512]{2,1,0:T(8,128)(2,1)}, u32[]{:S(2)}, u32[]{:S(2)}) %all-to-all-start.12) | async-done | bytes 1048608 | tf_op jit(solution)/shard_map/all_to_all | solution.py:105
  594.4 13.2 all-gather.65.cloned.1.call-done
  611.6 17.8 all-gather.43.cloned.1.call-done
  645.4 31.8 %all_to_all.192 = bf16[8,128,512]{2,1,0:T(8,128)(2,1)S(1)} all-to-all(bf16[8,128,512]{2,1,0:T(8,128)(2,1)} %bitcast.602), channel_id=1, replica_groups=mesh['dp'=8,'tensor'=4] {'dp'}, dimensions={0} | all-to-all | bytes 2097152 | tf_op jit(solution)/shard_map/all_to_all | solution.py:105
  687.4 29.5 %all_to_all.193 = bf16[8,128,512]{2,1,0:T(8,128)(2,1)S(1)} all-to-all(bf16[8,128,512]{2,1,0:T(8,128)(2,1)} %bitcast.603), channel_id=1, replica_groups=mesh['dp'=8,'tensor'=4] {'dp'}, dimensions={0} | all-to-all | bytes 2097152 | tf_op jit(solution)/shard_map/all_to_all | solution.py:105
  741.9 34.3 %while.116 = (s32[]{:T(128)}, bf16[3,512,2,64]{1,3,2,0:T(8,128)(2,1)S(1)}, f32[3,2,512]{2,1,0:T(2,128)S(1)}, s32[3]{0:T(128)S(1)}, s32[1536]{0:T(1024)S(1)}, /*i...) while((s32[]{:T(128)}, ...), condition=%wide.region_15.16_spmd, body=%wide.region_12.15_spmd.sunk | while | flops 426311680 | bytes 23119032 | solution.py:146
  809.8 54.9 %while.122 = (s32[]{:T(128)}, f32[1536,2,64]{0,2,1:T(8,128)S(1)}, f32[1536,2,64]{0,2,1:T(8,128)S(1)}, bf16[3,512,2,64]{1,3,2,0:T(8,128)(2,1)}, s32[3]{0:T(128)S(...) while((s32[]{:T(128)}, f32[1536,2,64]{0,2,1:T(8,128)S(1)}, ...), condition=%wide.region_95.96_spmd.clone, body=%wide.region_93.95_spmd.clone.sunk | while | flops 1027932160 | bytes 67933672 | solution.py:246
  883.2 29.0 %all_to_all.194 = bf16[8,128,512]{2,1,0:T(8,128)(2,1)S(1)} all-to-all(bf16[8,128,512]{2,1,0:T(8,128)(2,1)} %bitcast.604), channel_id=1, replica_groups=mesh['dp'=8,'tensor'=4] {'dp'}, dimensions={0} | all-to-all | bytes 2097152 | tf_op jit(solution)/shard_map/all_to_all | solution.py:105
  916.6 31.4 %reduce-scatter.31.cloned.1.call-done = f32[384,512]{1,0:T(8,128)} async-done(((f32[1536,512]{1,0:T(8,128)}), f32[384,512]{1,0:T(8,128)}) %reduce-scatter.31.cloned.1.call-update) | async-done | bytes 786448 | tf_op jit(solution)/shard_map/reduce_scatter | solution.py:165
  948.0 40.4 %reduce-scatter.23.cloned.1.call-done = f32[384,512]{1,0:T(8,128)} async-done(((f32[1536,512]{1,0:T(8,128)}), f32[384,512]{1,0:T(8,128)}) %reduce-scatter.23.cloned.1.call-update) | async-done | bytes 786448 | tf_op jit(solution)/shard_map/reduce_scatter | solution.py:165
  988.3 40.7 %reduce-scatter.43.cloned.1.call-done = f32[384,512]{1,0:T(8,128)} async-done(((f32[1536,512]{1,0:T(8,128)}), f32[384,512]{1,0:T(8,128)}) %reduce-scatter.43.cloned.1.call-update) | async-done | bytes 786448 | tf_op jit(solution)/shard_map/reduce_scatter | solution.py:260
  1053.9 57.9 %while.123 = (s32[]{:T(128)}, f32[1536,2,64]{0,2,1:T(8,128)S(1)}, f32[1536,2,64]{0,2,1:T(8,128)S(1)}, bf16[3,512,2,64]{1,3,2,0:T(8,128)(2,1)}, s32[3]{0:T(128)S(...) while((s32[]{:T(128)}, f32[1536,2,64]{0,2,1:T(8,128)S(1)}, ...), condition=%wide.region_101.102_spmd.clone, body=%wide.region_99.101_spmd.clone.sunk | while | flops 1027932160 | bytes 67933672 | solution.py:246
  1140.3 33.5 %reduce-scatter.47.cloned.1.call-done = f32[384,512]{1,0:T(8,128)} async-done(((f32[1536,512]{1,0:T(8,128)}), f32[384,512]{1,0:T(8,128)}) %reduce-scatter.47.cloned.1.call-update) | async-done | bytes 786448 | tf_op jit(solution)/shard_map/reduce_scatter | solution.py:260
  1176.7 37.4 %reduce-scatter.33.cloned.1.call-done = f32[384,512]{1,0:T(8,128)} async-done(((f32[1536,512]{1,0:T(8,128)}), f32[384,512]{1,0:T(8,128)}) %reduce-scatter.33.cloned.1.call-update) | async-done | bytes 786448 | tf_op jit(solution)/shard_map/reduce_scatter | solution.py:191
  1238.3 27.4 %all-gather.75.cloned.1.call-done = f32[1536,512]{1,0:T(8,128)} async-done(((f32[384,512]{1,0:T(8,128)}), f32[1536,512]{1,0:T(8,128)}) %all-gather.75.cloned.1.call-update) | async-done | bytes 3145744 | tf_op jit(solution)/shard_map/all_gather | solution.py:272
  1279.6 58.9 %while.121 = (s32[]{:T(128)}, f32[1536,2,64]{0,2,1:T(8,128)}, f32[1536,2,64]{0,2,1:T(8,128)S(1)}, bf16[3,512,2,64]{1,3,2,0:T(8,128)(2,1)}, s32[3]{0:T(128)S(1)},...) while((s32[]{:T(128)}, f32[1536,2,64]{0,2,1:T(8,128)}, ...), condition=%wide.region_89.90_spmd.clone, body=%wide.region_87.89_spmd.clone.sunk | while | flops 1027932160 | bytes 74225192 | solution.py:246
  1367.8 54.5 %while.120 = (s32[]{:T(128)}, f32[1536,2,64]{0,2,1:T(8,128)S(1)}, f32[1536,2,64]{0,2,1:T(8,128)S(1)}, bf16[3,512,2,64]{1,3,2,0:T(8,128)(2,1)}, s32[3]{0:T(128)S(...) while((s32[]{:T(128)}, f32[1536,2,64]{0,2,1:T(8,128)S(1)}, ...), condition=%wide.region_83.84_spmd.clone, body=%wide.region_81.83_spmd.clone.sunk | while | flops 1027932160 | bytes 67933672 | solution.py:246
  1455.6 36.1 %all-to-all-done.7 = f32[8,128,512]{2,1,0:T(8,128)} async-done(((f32[8,128,512]{2,1,0:T(8,128)}), f32[8,128,512]{2,1,0:T(8,128)}, u32[]{:S(2)}, u32[]{:S(2)}) %all-to-all-start.7) | async-done | bytes 2097184 | tf_op jit(solution)/shard_map/all_to_all | solution.py:277
  1507.8 36.1 %all-to-all-done.13 = f32[8,128,512]{2,1,0:T(8,128)} async-done(((f32[8,128,512]{2,1,0:T(8,128)}), f32[8,128,512]{2,1,0:T(8,128)}, u32[]{:S(2)}, u32[]{:S(2)}) %all-to-all-start.13) | async-done | bytes 2097184 | tf_op jit(solution)/shard_map/all_to_all | solution.py:280
  1568.8 27.2 %all-to-all-done.5 = f32[8,128,512]{2,1,0:T(8,128)} async-done(((f32[8,128,512]{2,1,0:T(8,128)}), f32[8,128,512]{2,1,0:T(8,128)}, u32[]{:S(2)}, u32[]{:S(2)}) %all-to-all-start.5) | async-done | bytes 2097184 | tf_op jit(solution)/shard_map/all_to_all | solution.py:277
  1622.9 25.3 %all-to-all-done.1 = f32[8,128,512]{2,1,0:T(8,128)} async-done(((f32[8,128,512]{2,1,0:T(8,128)}), f32[8,128,512]{2,1,0:T(8,128)}, u32[]{:S(2)}, u32[]{:S(2)}) %all-to-all-start.1) | async-done | bytes 2097184 | tf_op jit(solution)/shard_map/all_to_all | solution.py:277
  1677.1 51.0 %all-to-all-done.11 = f32[8,128,512]{2,1,0:T(8,128)} async-done(((f32[8,128,512]{2,1,0:T(8,128)}), f32[8,128,512]{2,1,0:T(8,128)}, u32[]{:S(2)}, u32[]{:S(2)}) %all-to-all-start.11) | async-done | bytes 2097184 | tf_op jit(solution)/shard_map/all_to_all | solution.py:280
  1771.6 71.2 %all-reduce.10.cloned.1.call-done = (f32[3,512,128]{1,2,0:T(8,128)}, f32[128,512]{1,0:T(8,128)}, f32[512,512]{1,0:T(8,128)}, f32[512,512]{1,0:T(8,128)}) async-done(((f32[3,512,128]{1,2,0:T(8,128)}, f32[128,512]{1,0:T(8,128)}, f32[512,512]{1,0:T(8,128)}, f32[512,512]{1,0:T(8,128)}), (f32[3,512,128]{1,2,0:T(8,128)}, f32[128,512]{1,0:T(8,128)}, f32[512,512]{1,0:T(8,128)}, ...) | async-done | bytes 3145744 | tf_op jit(solution)/shard_map/psum | solution.py:290
  1863.6 22.9 %all-reduce.12.cloned.1.call-done = (f32[4104]{0:T(1024)}, f32[4104]{0:T(1024)}, f32[4104]{0:T(1024)}, f32[4104]{0:T(1024)}) async-done(((f32[4104]{0:T(1024)}, f32[4104]{0:T(1024)}, f32[4104]{0:T(1024)}, f32[4104]{0:T(1024)}), (f32[4104]{0:T(1024)}, f32[4104]{0:T(1024)}, f32[4104]{0:T(1024)}, f32[4104]{0:T(1024)})) %all-reduce.12.cloned.1.call-update) | async-done | bytes 65680
  1889.9 37.5 %all-reduce.4 = (f32[2,128]{1,0:T(2,128)}, f32[1026]{0:T(1024)S(1)}, f32[512]{0:T(512)}) all-reduce(f32[2,128]{1,0:T(2,128)S(1)} %fusion.289, f32[1026]{0:T(1024)S(1)} %add_add_fusion, f32[512]{0:T(512)S(1)} %add_add_fusion.1), channel_id=1, replica_groups=mesh['dp'=8,'tensor'=4] {'dp'}, use_global_device_ids=true, to_apply=%region_113.114 | all-reduce | flops 1794 | bytes 14352 | tf_op jit(solution)/shard_map/psum | solution.py:290
  (1235 shorter events, 977.3 us)
Async XLA Ops:
  84.7 154.8 %all-to-all-start.4 = ((bf16[8,128,512]{2,1,0:T(8,128)(2,1)}), bf16[8,128,512]{2,1,0:T(8,128)(2,1)}, u32[]{:S(2)}, u32[]{:S(2)}) async-start(bf16[8,128,512]{2,1,0:T(8,128)(2,1)} %bitcast.598), calls=%async_computation.8 | async-start | bytes 2097152 | tf_op jit(solution)/shard_map/all_to_all | solution.py:102
  245.6 155.5 %all-gather.41.cloned.1.call-start = ((), (), s32[]{:S(2)}) async-start(), calls=%async_computation.42 | async-start | bytes 1966080 | tf_op jit(solution)/shard_map/all_gather | solution.py:122
  279.1 125.6 %all-gather.47.cloned.1.call-start = ((), (), s32[]{:S(2)}) async-start(), calls=%async_computation.47 | async-start | bytes 1966080 | tf_op jit(solution)/shard_map/all_gather | solution.py:122
  283.6 125.0 %all-gather.35.cloned.1.call-start = ((), (), s32[]{:S(2)}) async-start(), calls=%async_computation.37 | async-start | bytes 1966080 | tf_op jit(solution)/shard_map/all_gather | solution.py:122
  401.0 188.7 %reduce-scatter.21.cloned.1.call-start = ((), (), s32[]{:S(2)}) async-start(), calls=%async_computation.38 | async-start | bytes 3932160 | tf_op jit(solution)/shard_map/reduce_scatter | solution.py:149
  465.8 123.8 %reduce-scatter.25.cloned.1.call-start = ((), (), s32[]{:S(2)}) async-start(), calls=%async_computation.43 | async-start | bytes 3932160 | tf_op jit(solution)/shard_map/reduce_scatter | solution.py:149
  593.6 128.2 %reduce-scatter.41.cloned.1.call-start = ((), (), s32[]{:S(2)}) async-start(), calls=%async_computation.63 | async-start | bytes 3932160 | tf_op jit(solution)/shard_map/reduce_scatter | solution.py:191
  682.2 107.7 %all-gather.59.cloned.1.call-start = ((), (), s32[]{:S(2)}) async-start(), calls=%async_computation.57 | async-start | bytes 1966080 | tf_op jit(solution)/shard_map/all_gather | solution.py:179
  725.1 149.6 %reduce-scatter.45.cloned.1.call-start = ((), (), s32[]{:S(2)}) async-start(), calls=%async_computation.68 | async-start | bytes 3932160 | tf_op jit(solution)/shard_map/reduce_scatter | solution.py:191
  740.9 175.7 %reduce-scatter.17.cloned.1.call-start = ((), (), s32[]{:S(2)}) async-start(), calls=%async_computation.33 | async-start | bytes 3932160 | tf_op jit(solution)/shard_map/reduce_scatter | solution.py:149
  780.1 136.4 %reduce-scatter.27.cloned.1.call-start = ((), (), s32[]{:S(2)}) async-start(), calls=%async_computation.45 | async-start | bytes 3932160 | tf_op jit(solution)/shard_map/reduce_scatter | solution.py:165
  785.0 163.0 %reduce-scatter.31.cloned.1.call-start = ((), (), s32[]{:S(2)}) async-start(), calls=%async_computation.50 | async-start | bytes 3932160 | tf_op jit(solution)/shard_map/reduce_scatter | solution.py:165
  789.8 198.6 %reduce-scatter.23.cloned.1.call-start = ((), (), s32[]{:S(2)}) async-start(), calls=%async_computation.40 | async-start | bytes 3932160 | tf_op jit(solution)/shard_map/reduce_scatter | solution.py:165
  806.7 222.3 %reduce-scatter.43.cloned.1.call-start = ((), (), s32[]{:S(2)}) async-start(), calls=%async_computation.65 | async-start | bytes 3932160 | tf_op jit(solution)/shard_map/reduce_scatter | solution.py:260
  874.6 175.7 %all-gather.73.cloned.1.call-start = ((), (), s32[]{:S(2)}) async-start(), calls=%async_computation.69 | async-start | bytes 1966080 | tf_op jit(solution)/shard_map/all_gather | solution.py:207
  878.0 243.6 %all-gather.53.cloned.1.call-start = ((), (), s32[]{:S(2)}) async-start(), calls=%async_computation.52 | async-start | bytes 1966080 | tf_op jit(solution)/shard_map/all_gather | solution.py:179
  916.5 209.3 %all-gather.31.cloned.1.call-start = ((), (), s32[]{:S(2)}) async-start(), calls=%async_computation.34 | async-start | bytes 1966080 | tf_op jit(solution)/shard_map/all_gather | solution.py:160
  1036.0 100.0 %reduce-scatter.37.cloned.1.call-start = ((), (), s32[]{:S(2)}) async-start(), calls=%async_computation.58 | async-start | bytes 3932160 | tf_op jit(solution)/shard_map/reduce_scatter | solution.py:191
  1040.6 133.2 %reduce-scatter.47.cloned.1.call-start = ((), (), s32[]{:S(2)}) async-start(), calls=%async_computation.70 | async-start | bytes 3932160 | tf_op jit(solution)/shard_map/reduce_scatter | solution.py:260
  1136.0 99.5 %all-gather.61.cloned.1.call-start = ((), (), s32[]{:S(2)}) async-start(), calls=%async_computation.59 | async-start | bytes 1966080 | tf_op jit(solution)/shard_map/all_gather | solution.py:207
  1140.2 125.5 %all-gather.75.cloned.1.call-start = ((), (), s32[]{:S(2)}) async-start(), calls=%async_computation.71 | async-start | bytes 3932160 | tf_op jit(solution)/shard_map/all_gather | solution.py:272
  1176.1 175.3 %all-gather.39.cloned.1.call-start = ((), (), s32[]{:S(2)}) async-start(), calls=%async_computation.41 | async-start | bytes 3932160 | tf_op jit(solution)/shard_map/all_gather | solution.py:271
  1176.7 181.9 %all-gather.55.cloned.1.call-start = ((), (), s32[]{:S(2)}) async-start(), calls=%async_computation.54 | async-start | bytes 1966080 | tf_op jit(solution)/shard_map/all_gather | solution.py:207
  1217.4 212.9 %all-gather.51.cloned.1.call-start = ((), (), s32[]{:S(2)}) async-start(), calls=%async_computation.51 | async-start | bytes 3932160 | tf_op jit(solution)/shard_map/all_gather | solution.py:271
  1218.2 230.2 %all-gather.69.cloned.1.call-start = ((), (), s32[]{:S(2)}) async-start(), calls=%async_computation.66 | async-start | bytes 3932160 | tf_op jit(solution)/shard_map/all_gather | solution.py:272
  1218.7 277.4 %reduce-scatter.19.cloned.1.call-start = ((), (), s32[]{:S(2)}) async-start(), calls=%async_computation.35 | async-start | bytes 3932160 | tf_op jit(solution)/shard_map/reduce_scatter | solution.py:165
  1223.7 276.2 %all-gather.45.cloned.1.call-start = ((), (), s32[]{:S(2)}) async-start(), calls=%async_computation.46 | async-start | bytes 3932160 | tf_op jit(solution)/shard_map/all_gather | solution.py:271
  1278.6 270.2 %reduce-scatter.39.cloned.1.call-start = ((), (), s32[]{:S(2)}) async-start(), calls=%async_computation.60 | async-start | bytes 3932160 | tf_op jit(solution)/shard_map/reduce_scatter | solution.py:260
  1366.7 182.1 %reduce-scatter.35.cloned.1.call-start = ((), (), s32[]{:S(2)}) async-start(), calls=%async_computation.55 | async-start | bytes 3932160 | tf_op jit(solution)/shard_map/reduce_scatter | solution.py:260
  1652.6 190.3 %all-reduce.10.cloned.1.call-start = ((), (), s32[]{:S(2)}) async-start(), calls=%async_computation.72 | async-start | bytes 6291456 | tf_op jit(solution)/shard_map/psum | solution.py:290
  1728.1 207.5 %all-to-all-start.9 = ((f32[8,128,512]{2,1,0:T(8,128)}), f32[8,128,512]{2,1,0:T(8,128)}, u32[]{:S(2)}, u32[]{:S(2)}) async-start(f32[8,128,512]{2,1,0:T(8,128)} %bitcast.129), calls=%async_computation.19 | async-start | bytes 4194304 | tf_op jit(solution)/shard_map/all_to_all | solution.py:280
  1733.6 153.0 %all-reduce.12.cloned.1.call-start = ((), (), s32[]{:S(2)}) async-start(), calls=%async_computation.73 | async-start | bytes 163840
  (270 other events, 6784.5 us)
Sparse Core Ops, SparseCore 0:
  250.4 23.1 all-gather.40
  283.7 21.0 all-gather.46
  362.6 21.0 all-gather.34
  465.9 37.9 reduce-scatter.20
  506.5 37.9 reduce-scatter.24
  547.6 37.9 reduce-scatter.28
  639.8 37.9 reduce-scatter.40
  743.9 19.7 all-gather.36
  787.7 37.9 reduce-scatter.44
  828.2 38.0 reduce-scatter.16
  869.2 38.0 reduce-scatter.26
  910.0 37.9 reduce-scatter.30
  950.4 37.9 reduce-scatter.22
  991.1 37.9 reduce-scatter.42
  1030.6 19.6 all-gather.72
  1072.9 19.6 all-gather.30
  1095.2 37.9 reduce-scatter.36
  1135.8 37.9 reduce-scatter.46
  1176.2 37.9 reduce-scatter.32
  1237.1 28.5 all-gather.74
  1267.2 28.5 all-gather.38
  1319.3 28.5 all-gather.50
  1350.0 28.5 all-gather.68
  1381.2 37.9 reduce-scatter.18
  1421.4 28.5 all-gather.44
  1452.4 37.9 reduce-scatter.38
  1492.9 37.9 reduce-scatter.34
  1533.1 28.5 all-gather.32
  1563.0 28.5 all-gather.62
  1607.8 29.5 all-gather.56
  1669.9 172.9 all-reduce.9
  1857.7 28.7 all-reduce.11
  (10 shorter events, 191.7 us)
where the time goes:
time: 1970 us; the launch traced here: 1960 us
  waiting for transfers between devices  571 us (29%)
  other arithmetic  436 us (22%)
  local copies, waits for them, and re-layouts  362 us (18%)
  matrix products  297 us (15%)
  blocking collectives  128 us (6%)
  starting transfers between devices  75.8 us (4%)
  loops' own time  69.1 us (4%)
    scatter-add x4, other arithmetic, per_device(): jnp.nonzero(owners == group_id, size=tok_rows)[0].astype(jnp.int32)  228 us
    all_to_all x3, blocking collectives, per_device(): lax.all_to_all(cotangent[micro_index][send_rows], 'dp', split_axis=0, con...  90.2 us
    all_to_all x4, waiting for transfers between devices, per_device(): lax.all_to_all(output_all[arrival_slots], 'dp', split_axis=0, concat_axis...  88.6 us
    all_to_all x4, waiting for transfers between devices, per_device(): lax.all_to_all(grad_input_all[arrival_slots], 'dp', split_axis=0, concat_...  87.1 us
    reduce_scatter x4, waiting for transfers between devices, per_device(): lax.psum_scatter(jnp.einsum('cse,cde->sd', grad_qkv, qkv_weight, preferre...  74.2 us
    reduce_scatter x4, waiting for transfers between devices, per_device(): lax.psum_scatter(jnp.dot(lax.slice_in_dim(activated, 0, own_rows * lax.ax...  71.8 us
    psum x1, waiting for transfers between devices, per_device(): lax.psum((qkv_grad_sum, qv_bias_sum, out_grad_sum, up_grad_sum, up_bias_s...  71.2 us
    dot_general x24, matrix products, masked_scores(): jnp.einsum('qhe,khe->hqk', query_block, key_heads, preferred_element_type...  60.4 us
  transfers between devices with their start and end apart: 55, of which 21 were waited for; matrix products, arithmetic and copies ran while one was open for 47% of the time, Pallas kernels for 0%

commit v1 on v0

v1 whole, which is shorter than its diff:
```python
import functools

import jax
import jax.numpy as jnp
from jax import lax
from jax.experimental import pallas as pl
from jax.experimental.pallas import tpu as pltpu
from jax.sharding import PartitionSpec as P

HEAD_SIZE = 64
LANES = 128
QT = 256
BF = jnp.bfloat16
F32 = jnp.float32
I32 = jnp.int32
NEG = -1e30
VMEM_LIMIT = 56 * 1024 * 1024
GELU_A = 0.7978845608028654
GELU_B = 0.044715

NN = (((1,), (0,)), ((), ()))
NT = (((1,), (1,)), ((), ()))
TN = (((0,), (0,)), ((), ()))


def dot(a, b, dims=NN):
    return lax.dot_general(a, b, dims, preferred_element_type=F32)


def iota(shape, dim):
    return lax.broadcasted_iota(I32, shape, dim)


def params(limit=VMEM_LIMIT):
    return pltpu.CompilerParams(vmem_limit_bytes=limit)


def cost(flops, nbytes, trans=0):
    return pl.CostEstimate(flops=int(flops), bytes_accessed=int(nbytes), transcendentals=int(trans))


def vmem(n):
    return [pl.BlockSpec(memory_space=pltpu.VMEM)] * n


def smem():
    return pl.BlockSpec(memory_space=pltpu.SMEM)


def one_hot_rows(row, count):
    return (iota((count, row.shape[1]), 0) == row).astype(F32).astype(BF)


def one_hot_cols(col, count):
    return (iota((col.shape[0], count), 1) == col).astype(F32).astype(BF)


def route_kernel(groups, ids_ref, src_ref, x_ref, xs_ref, srow_ref, scol_ref, hot_ref):
    me, micro = ids_ref[0], ids_ref[1]
    rows = x_ref.shape[1]
    chunks = rows // LANES
    share = rows // groups
    sub_hi = iota((chunks, rows), 0)
    sub_lo = iota((LANES, rows), 0)

    def gather_group(g, total):
        value = src_ref[pl.ds(micro, 1), pl.ds(pl.multiple_of(g * rows, LANES), rows)] - me * rows
        inside = (value >= 0) & (value < rows)
        high = jnp.where(inside, value // LANES, -1)
        low = jnp.where(inside, value % LANES, -1)
        hot_high = jnp.where(high == sub_hi, (g + 1).astype(F32), 0.0).astype(BF)
        hot_low = (low == sub_lo).astype(F32).astype(BF)
        return total + dot(hot_high, hot_low, NT)

    dest = lax.fori_loop(0, groups, gather_group, jnp.zeros((chunks, LANES), F32)).astype(I32) - 1
    before = (iota((LANES, LANES), 0) < iota((LANES, LANES), 1)).astype(F32).astype(BF)
    width = max(groups, 8)
    carry = jnp.zeros((width, 1), F32)
    for c in range(chunks):
        g_row = dest[c : c + 1, :]
        hot = (iota((width, LANES), 0) == g_row).astype(F32)
        ranks = dot(hot.astype(BF), before) + carry
        carry = carry + jnp.sum(hot, axis=1, keepdims=True)
        place = g_row * share + jnp.sum(hot * ranks, axis=0, keepdims=True).astype(I32)
        srow_ref[c : c + 1, :] = place
        spread = jnp.broadcast_to(place.astype(F32), (LANES, LANES))
        scol_ref[c * LANES : (c + 1) * LANES, :] = spread.T.astype(I32)
        hot_ref[:, c * LANES : (c + 1) * LANES] = one_hot_rows(place, rows)
    xs_ref[...] = dot(hot_ref[...], x_ref[0]).astype(BF)


def second_kernel(ids_ref, src_ref, g_ref, srow_ref, gs_ref, arow_ref, acol_ref, hot_ref):
    me, micro = ids_ref[0], ids_ref[1]
    rows = g_ref.shape[1]
    for c in range(rows // LANES):
        hot_ref[:, c * LANES : (c + 1) * LANES] = one_hot_rows(srow_ref[c : c + 1, :], rows)
    gs_ref[...] = dot(hot_ref[...], g_ref[0]).astype(BF)
    own = src_ref[pl.ds(micro, 1), pl.ds(pl.multiple_of(me * rows, LANES), rows)].astype(F32)
    for c in range(rows // LANES):
        piece = own[:, c * LANES : (c + 1) * LANES]
        column = jnp.broadcast_to(piece, (LANES, LANES)).T[:, 0:1]
        count = jnp.sum((own < column).astype(F32), axis=1, keepdims=True)
        spread = jnp.broadcast_to(count, (LANES, LANES))
        acol_ref[c * LANES : (c + 1) * LANES, :] = spread.astype(I32)
        arow_ref[0:1, c * LANES : (c + 1) * LANES] = spread.T[0:1, :].astype(I32)


def starts_of(len_ref, index):
    start = jnp.zeros_like(index)
    first = jnp.int32(0)
    for j in range(len_ref.shape[0] - 1):
        first = first + len_ref[j]
        start = jnp.where(index >= first, first, start)
    return start


def attend_kernel(
    ids_ref, len_ref, alpha_ref, arr_ref, acol_ref, wa_ref, wo0_ref, wo1_ref, wo2_ref, wo3_ref,
    b0_ref, b1_ref, b2_ref, b3_ref, ob_ref,
    x_ref, q_ref, k_ref, v_ref, o_ref, l_ref, h_ref, attn_ref, wcat_ref, wo_ref, bias_ref,
    hot_ref,
):
    pieces, _, width, lanes = wa_ref.shape
    rows = arr_ref.shape[0]
    tensor = ids_ref[1]
    for j, (w, b) in enumerate(((wo0_ref, b0_ref), (wo1_ref, b1_ref), (wo2_ref, b2_ref), (wo3_ref, b3_ref))):
        slot = lax.bitwise_xor(tensor, j)
        wo_ref[slot] = w[...]
        bias_ref[slot] = b[...].astype(F32)
    for r in range(pieces):
        for c in range(3):
            wcat_ref[:, c * width + r * lanes : c * width + (r + 1) * lanes] = wa_ref[r, c]
    hot_ref[...] = one_hot_cols(acol_ref[:, 0:1], rows)
    x_ref[...] = dot(hot_ref[...], arr_ref[...]).astype(BF)
    for c, out in enumerate((q_ref, k_ref, v_ref)):
        proj = dot(x_ref[...], wcat_ref[:, c * width : (c + 1) * width])
        for r in range(pieces):
            part = proj[:, r * lanes : (r + 1) * lanes]
            if c != 1:
                part = part + bias_ref[r, c // 2 : c // 2 + 1, :]
            part = part.astype(BF)
            if c == 0:
                part = part * jnp.asarray(HEAD_SIZE**-0.5, BF)
            out[r] = part
    heads = lanes // HEAD_SIZE

    def pair(p, _):
        for i in range(rows // QT):
            n = (i + 1) * QT
            q_index = i * QT + iota((QT, 1), 0)
            start = starts_of(len_ref, q_index)
            k_index = iota((QT, n), 1)
            allowed = (k_index >= start) & (k_index <= q_index)
            q = q_ref[p, i * QT : n, :]
            lane = iota((QT, lanes), 1) // HEAD_SIZE
            k, v = k_ref[p, 0:n, :], v_ref[p, 0:n, :]
            mixed = jnp.zeros((QT, lanes), F32)
            for e in range(heads):
                scores = dot(jnp.where(lane == e, q, jnp.zeros_like(q)), k, NT)
                scores = jnp.where(allowed, scores, NEG)
                top = jnp.max(scores, axis=1, keepdims=True)
                weights = jnp.exp(scores - top)
                total = jnp.sum(weights, axis=1, keepdims=True)
                low = (weights * (1.0 / total)).astype(BF)
                mixed = jnp.where(lane == e, dot(low, v), mixed)
                log_total = jnp.broadcast_to(top + jnp.log(total), (QT, LANES))
                l_ref[p, e : e + 1, i * QT : n] = log_total.T[0:1, :]
            o_ref[p, i * QT : n, :] = mixed.astype(BF)
        return 0

    lax.fori_loop(0, pieces, pair, 0)
    attn = ob_ref[...].astype(F32)
    for r in range(pieces):
        attn = attn + dot(o_ref[r], wo_ref[r])
    attn_ref[...] = attn
    h_ref[...] = x_ref[...].astype(F32) + alpha_ref[0] * attn


def feed_kernel(
    ids_ref, alpha_ref, arr_ref, acol_ref, arow_ref, h_ref, attn_ref, o_ref, bias_ref, wo_ref, wu_ref, wd_ref, db_ref,
    ys_ref, go_ref, gh_ref, keep_ref, send_ref, small_ref,
    hot_ref, low_ref, gf_ref, f_ref,
):
    me, tensor = ids_ref[0], ids_ref[1]
    pieces, width, units = wu_ref.shape
    rows = arr_ref.shape[0]
    lanes = bias_ref.shape[2]
    blocks = keep_ref.shape[1]
    hot_ref[...] = one_hot_cols(acol_ref[:, 0:1], rows)
    grad = dot(hot_ref[...], arr_ref[...])
    gh_ref[...] = grad
    gf_ref[...] = (alpha_ref[1] * grad).astype(BF)
    low_ref[...] = h_ref[...].astype(BF)
    f_ref[...] = jnp.broadcast_to(db_ref[...].astype(F32), f_ref.shape)

    def place(r, first, value):
        slot = lax.bitwise_xor(r, tensor)
        count = value.shape[0] // blocks
        for parity, out in ((0, keep_ref), (1, send_ref)):

            @pl.when(slot % 2 == parity)
            def _():
                for b in range(blocks):
                    out[slot // 2, lax.bitwise_xor(me % blocks, b), first : first + count, :] = value[b * count : (b + 1) * count]

    def piece(r, _):
        bias = jnp.concatenate([bias_ref[r, 2 + b : 3 + b, :] for b in range(units // lanes)], axis=1)
        z = dot(low_ref[...], wu_ref[r]) + bias
        square = z * z
        tanh = jnp.tanh(z * (GELU_A + (GELU_A * GELU_B) * square))
        half = 0.5 * z
        act = (half + half * tanh).astype(BF)
        slope = (0.5 + 0.5 * tanh) + half * (1.0 - tanh * tanh) * (GELU_A + (3 * GELU_A * GELU_B) * square)
        f_ref[...] += dot(act, wd_ref[r])
        gz_full = dot(gf_ref[...], wd_ref[r], NT) * slope
        gz = gz_full.astype(BF)
        gh_ref[...] += dot(gz, wu_ref[r], NT)
        place(r, 0, dot(low_ref[...], gz, TN).astype(BF))
        place(r, width // blocks, dot(act, gf_ref[...], TN).astype(BF))
        small_ref[pl.ds(r, 1), :] = jnp.sum(gz.astype(F32), axis=0, keepdims=True)
        return 0

    lax.fori_loop(0, pieces, piece, 0)
    branch = f_ref[...]
    y = (h_ref[...] + alpha_ref[1] * branch).astype(BF)
    grad_hidden = gh_ref[...]
    ga = (alpha_ref[0] * grad_hidden).astype(BF)
    small_ref[4:5, :] = jnp.sum(ga.astype(F32), axis=0, keepdims=True)
    small_ref[5:6, :] = jnp.sum(gf_ref[...].astype(F32), axis=0, keepdims=True)
    small_ref[6:7, :] = jnp.sum(grad_hidden * attn_ref[...], axis=0, keepdims=True)
    for r in range(pieces):
        go_ref[r] = dot(ga, wo_ref[r], NT).astype(BF)
        place(jnp.int32(r), (width + units) // blocks, dot(o_ref[r], ga, TN).astype(BF))
    for c in range(rows // LANES):
        hot_ref[c * LANES : (c + 1) * LANES, :] = (iota((LANES, rows), 0) + c * LANES == arow_ref[0:1, :]).astype(F32).astype(BF)
    grad_tokens = dot(one_hot_cols(acol_ref[:, 0:1], rows), arr_ref[...])
    small_ref[7:8, :] = jnp.sum(grad_tokens * branch, axis=0, keepdims=True)
    ys_ref[...] = dot(hot_ref[...], y).astype(BF)


def back_kernel(
    pairs, len_ref, q_ref, k_ref, v_ref, go_ref, l_ref,
    grad_ref,
    gk_acc, gv_acc,
):
    _, rows, lanes = q_ref.shape
    heads = lanes // HEAD_SIZE
    scale = HEAD_SIZE**-0.5

    def pair(p, _):
        gk_acc[...] = jnp.zeros_like(gk_acc)
        gv_acc[...] = jnp.zeros_like(gv_acc)
        for i in range(rows // QT):
            n = (i + 1) * QT
            q_index = i * QT + iota((1, QT), 1)
            start = starts_of(len_ref, q_index)
            k_index = iota((n, QT), 0)
            allowed = (k_index >= start) & (k_index <= q_index)
            q, go = q_ref[p, i * QT : n, :], go_ref[p, i * QT : n, :]
            k, v = k_ref[p, 0:n, :], v_ref[p, 0:n, :]
            lane_q = iota((QT, lanes), 1) // HEAD_SIZE
            gq = jnp.zeros((QT, lanes), F32)
            for e in range(heads):
                q_e = jnp.where(lane_q == e, q, jnp.zeros_like(q))
                go_e = jnp.where(lane_q == e, go, jnp.zeros_like(go))
                scores = dot(k, q_e, NT) - l_ref[p, e : e + 1, i * QT : n]
                weights = jnp.exp(jnp.where(allowed, scores, NEG))
                grad_weights = dot(v, go_e, NT)
                inner = jnp.sum(weights * grad_weights, axis=0, keepdims=True)
                grad_scores = (weights * (grad_weights - inner)).astype(BF)
                gv_acc[0:n, :] += dot(weights.astype(BF), go_e)
                gk_acc[0:n, :] += dot(grad_scores, q_e)
                gq = jnp.where(lane_q == e, dot(grad_scores, k, TN), gq)
            grad_ref[0, p - pairs[0], i * QT : n, :] = (gq * scale).astype(BF)
        grad_ref[1, p - pairs[0]] = gk_acc[...].astype(BF)
        grad_ref[2, p - pairs[0]] = gv_acc[...].astype(BF)
        return 0

    lax.fori_loop(pairs[0], pairs[1], pair, 0)


def last_kernel(
    ids_ref, x_ref, grad_a_ref, grad_b_ref, gh_ref, wcat_ref, arow_ref, small1_ref,
    gxs_ref, keep_ref, send_ref, small_ref,
    grad_ref, hot_ref,
):
    me, tensor = ids_ref[0], ids_ref[1]
    rows, width = x_ref.shape
    half, lanes = grad_a_ref.shape[1], grad_a_ref.shape[3]
    pieces = 2 * half
    blocks = keep_ref.shape[1]
    for c in range(3):
        for r in range(pieces):
            first = c * width + r * lanes
            grad_ref[:, first : first + lanes] = grad_a_ref[c, r] if r < half else grad_b_ref[c, r - half]
    gx = gh_ref[...] + dot(grad_ref[...], wcat_ref[...], NT)
    for c in range(rows // LANES):
        hot_ref[c * LANES : (c + 1) * LANES, :] = (iota((LANES, rows), 0) + c * LANES == arow_ref[0:1, :]).astype(F32).astype(BF)
    gxs_ref[...] = dot(hot_ref[...], gx.astype(BF)).astype(BF)
    count = width // blocks
    small_ref[0:8, :] = small1_ref[...]
    small_ref[8:16, :] = jnp.zeros((8, width), F32)
    for c in range(3):
        grad_w = dot(x_ref[...], grad_ref[:, c * width : (c + 1) * width], TN).astype(BF)
        for r in range(pieces):
            slot = lax.bitwise_xor(jnp.int32(r), tensor)
            for parity, out in ((0, keep_ref), (1, send_ref)):

                @pl.when(slot % 2 == parity)
                def _():
                    for b in range(blocks):
                        out[slot // 2, lax.bitwise_xor(me % blocks, b), c * count : (c + 1) * count, :] = grad_w[
                            b * count : (b + 1) * count, r * lanes : (r + 1) * lanes
                        ]

        if c != 1:
            row = 8 + c // 2
            small_ref[row : row + 1, :] = jnp.sum(
                grad_ref[:, c * width : (c + 1) * width].astype(F32), axis=0, keepdims=True
            )


def parted_kernel(axis, keep_ref, got_ref, *refs):
    outs = refs[-2:]
    for i in range(keep_ref.shape[0]):
        for b in range(keep_ref.shape[1]):
            total = (keep_ref[i, b].astype(F32) + got_ref[i, b].astype(F32)).astype(BF)
            if axis == 0:
                outs[i][b] = total
            else:
                outs[b % 2][i, b // 2] = total


def joined_kernel(keep_ref, got_ref, *refs):
    for b in range(keep_ref.shape[0]):
        total = (keep_ref[b].astype(F32) + got_ref[b].astype(F32)).astype(BF)
        refs[-keep_ref.shape[0] + b][...] = total


def sum_kernel(count, *refs):
    total = refs[0][...].astype(F32)
    for r in refs[1:count]:
        total = total + r[...].astype(F32)
    refs[-1][...] = total.astype(refs[-1].dtype)


def spread_first_kernel(count, ids_ref, *refs):
    blocks, (up_ref, down_ref, out_ref) = refs[:count], refs[-3:]
    for j, ref in enumerate(blocks):
        slot = lax.bitwise_xor(ids_ref[0] % count, j)
        first = 0
        for out in (up_ref, down_ref, out_ref):
            size = out.shape[0] // count
            out[pl.ds(pl.multiple_of(slot * size, 8), size), :] = ref[first : first + size, :].astype(F32)
            first += size


def spread_second_kernel(count, ids_ref, *refs):
    out_ref = refs[-1]
    size = out_ref.shape[1] // count
    for j, ref in enumerate(refs[:count]):
        slot = lax.bitwise_xor(ids_ref[0] % count, j)
        for c in range(3):
            out_ref[c, pl.ds(pl.multiple_of(slot * size, 8), size), :] = ref[c * size : (c + 1) * size, :].astype(F32)


def widen_kernel(ids_ref, *refs):
    out_ref, step = refs[-1], pl.program_id(0)
    for j, ref in enumerate(refs[:4]):

        @pl.when(step == j)
        def _():
            out_ref[0] = ref[...].astype(F32)


def settle_kernel(r_ref, scol_ref, out_ref):
    out_ref[...] = dot(one_hot_cols(scol_ref[:, 0:1], r_ref.shape[0]), r_ref[...]).astype(BF)


def shape(dims, kind):
    return jax.ShapeDtypeStruct(dims, kind)


def call(kernel, ins, outs, scratch=(), deps=(), flops=1e6, nbytes=4 << 20, scalars=0):
    n_in, n_dep = len(ins), len(deps)

    def body(*refs):
        kernel(*refs[:n_in], *refs[n_in + n_dep :])

    return pl.pallas_call(
        body,
        out_shape=list(outs),
        in_specs=[smem()] * scalars + vmem(n_in - scalars) + [pl.BlockSpec(memory_space=pl.ANY)] * n_dep,
        out_specs=vmem(len(outs)),
        scratch_shapes=list(scratch),
        compiler_params=params(),
        cost_estimate=cost(flops, nbytes),
    )(*ins, *deps)


def per_device(
    block_input, cotangent, source, seq_lengths, qkv_weight, qv_bias, out_weight, out_bias,
    up_weight, up_bias, down_weight, down_bias, rezero_alphas,
):
    micros, rows, width = block_input.shape
    groups = lax.axis_size("dp")
    tensors = lax.axis_size("tensor")
    lanes = qkv_weight.shape[2]
    units = up_weight.shape[1]
    blocks = min(groups, 8)
    me, tensor = lax.axis_index("dp"), lax.axis_index("tensor")
    ids = jnp.stack([me, tensor]).astype(I32)
    lengths = lax.dynamic_index_in_dim(seq_lengths, tensor, 0, keepdims=False)[0]

    def across(axis, bit, value):
        count = tensors if axis == "tensor" else groups
        return lax.ppermute(value, axis, [(i, i ^ bit) for i in range(count)])

    def four(value):
        far = across("tensor", 2, value)
        return value, across("tensor", 1, value), far, across("tensor", 1, far)

    wa = lax.all_gather(qkv_weight, "tensor", axis=0)
    wu = lax.all_gather(up_weight, "tensor", axis=0)
    wd = lax.all_gather(down_weight, "tensor", axis=0)
    wo4 = four(out_weight)
    bias4 = four(jnp.concatenate([qv_bias, up_bias.reshape(units // lanes, lanes), jnp.zeros((2, lanes), BF)], axis=0))

    def by_micro(kernel, n_whole, out_shape, scratch):
        return pl.pallas_call(
            kernel,
            out_shape=out_shape,
            grid_spec=pltpu.PrefetchScalarGridSpec(
                num_scalar_prefetch=1,
                grid=(1,),
                in_specs=[
                    pl.BlockSpec(source.shape, lambda i, s: (0, 0)),
                    pl.BlockSpec((1, rows, width), lambda i, s: (s[1], 0, 0)),
                ]
                + [pl.BlockSpec((rows // LANES, LANES), lambda i, s: (0, 0))] * n_whole,
                out_specs=[pl.BlockSpec(o.shape, lambda i, s: (0, 0)) for o in out_shape],
                scratch_shapes=scratch,
            ),
            compiler_params=params(),
            cost_estimate=cost(2 * rows * rows * width, 4 << 20),
        )

    hot = pltpu.VMEM((rows, rows), BF)
    xs, srow, scol = by_micro(
        functools.partial(route_kernel, groups), 0,
        [shape((rows, width), BF), shape((rows // LANES, LANES), I32), shape((rows, LANES), I32)], [hot],
    )(ids, source, block_input)

    def exchange(rows_out):
        return lax.all_to_all(rows_out.reshape(groups, rows // groups, width), "dp", 0, 0, tiled=True).reshape(rows, width)

    arr_x = exchange(xs)
    gs, arow, acol = by_micro(
        second_kernel, 1,
        [shape((rows, width), BF), shape((8, rows), I32), shape((rows, LANES), I32)], [hot],
    )(ids, source, cotangent, srow)
    arr_g = exchange(gs)

    heads3 = [shape((tensors, rows, lanes), BF)] * 4
    x, q, k, v, o, logs, h, attn, wcat, wo, bias = call(
        attend_kernel,
        (ids, lengths, rezero_alphas, arr_x, acol, wa, *wo4, *bias4, out_bias.reshape(1, width)),
        [shape((rows, width), BF), *heads3, shape((tensors, 8, rows), F32),
         shape((rows, width), F32), shape((rows, width), F32), shape((width, 3 * width), BF),
         shape((tensors, lanes, width), BF), shape((tensors, 8, lanes), F32)],
        [hot], scalars=3, flops=27e9, nbytes=16 << 20,
    )

    bundle = (width + units + lanes) // blocks
    part = shape((tensors // 2, blocks, bundle, width), BF)
    ys, go, gh, keep1, send1, small1 = call(
        feed_kernel,
        (ids, rezero_alphas, arr_g, acol, arow, h, attn, o, bias, wo, wu, wd, down_bias.reshape(1, width)),
        [shape((rows, width), BF), shape((tensors, rows, lanes), BF), shape((rows, width), F32), part, part,
         shape((8, width), F32)],
        [hot, pltpu.VMEM((rows, width), BF), pltpu.VMEM((rows, width), BF), pltpu.VMEM((rows, width), F32)],
        scalars=2, flops=31e9, nbytes=24 << 20,
    )
    arr_y = exchange(ys)
    got = across("tensor", 1, send1)

    def back(first, last, deps):
        return call(
            functools.partial(back_kernel, (first, last)), (lengths, q, k, v, go, logs),
            [shape((3, last - first, rows, lanes), BF)], [pltpu.VMEM((rows, lanes), F32)] * 2,
            scalars=1, flops=14e9, nbytes=8 << 20, deps=deps,
        )[0]

    half = tensors // 2

    def by_core(keep, got, deps):
        k_shape = shape((keep.shape[0], blocks // 2, *keep.shape[2:]), BF)
        return call(functools.partial(parted_kernel, 1), (keep, got), [k_shape, k_shape], deps=deps)

    def by_low(keep, got, deps):
        k_shape = shape(keep.shape[1:], BF)
        return call(functools.partial(parted_kernel, 0), (keep, got), [k_shape, k_shape], deps=deps)

    def by_far(keep, got, deps):
        return call(joined_kernel, (keep, got), [shape(keep.shape[1:], BF)] * (blocks // 2), deps=deps)

    def high(value):
        return [across("dp", 2 * j, v) for j, v in enumerate(value) if j]

    def total(values, kind, deps=()):
        return call(functools.partial(sum_kernel, len(values)), values, [shape(values[0].shape, kind)], deps=deps)[0]

    def rest(value, kind):
        bit = blocks
        while bit < groups:
            value = total((value, across("dp", bit, value)), kind)
            bit *= 2
        return value

    def gather(own):
        even = [own] + [across("dp", 2 * j, own) for j in range(1, blocks // 2)]
        odd = [across("dp", 1, e) for e in even]
        return [b for pair in zip(even, odd) for b in pair]

    grad_a = back(0, half, (keep1,))
    keep1, send1 = by_core(keep1, got, (grad_a,))
    got = across("dp", 1, send1)
    grad_b = back(half, tensors, (keep1,))

    def settle(rows_back, deps):
        return call(settle_kernel, (rows_back, scol), [shape((rows, width), BF)], deps=deps, flops=1e9)[0]

    def widen(four_parts):
        return pl.pallas_call(
            widen_kernel,
            out_shape=shape((tensors, rows, width), F32),
            grid_spec=pltpu.PrefetchScalarGridSpec(
                num_scalar_prefetch=1,
                grid=(tensors,),
                in_specs=[pl.BlockSpec((rows, width), lambda i, s: (0, 0))] * 4,
                out_specs=pl.BlockSpec((1, rows, width), lambda i, s: (lax.bitwise_xor(s[1], i), 0, 0)),
            ),
            compiler_params=params(),
            cost_estimate=cost(1e6, 12 << 20),
        )(ids, *four_parts)

    y_own = settle(arr_y, (grad_b,))
    y4 = four(y_own)
    share = (3 * width) // blocks
    part = shape((half, blocks, share, lanes), BF)
    gxs, keep2, send2, small = call(
        last_kernel, (ids, x, grad_a, grad_b, gh, wcat, arow, small1),
        [shape((rows, width), BF), part, part, shape((16, width), F32)],
        [pltpu.VMEM((rows, 3 * width), BF), hot], scalars=1, flops=7e9, nbytes=8 << 20, deps=(y_own,),
    )
    arr_gx = exchange(gxs)
    got2 = across("tensor", 1, send2)
    got3 = across("tensor", 1, small)
    keep1, send1 = by_low(keep1, got, (gxs,))
    got = across("tensor", 2, send1)
    keep2, send2 = by_core(keep2, got2, (keep1,))
    got2 = across("dp", 1, send2)
    small = total((small, got3), F32)
    got3 = across("dp", 1, small)
    blocks1 = call(joined_kernel, (keep1, got), [shape(keep1.shape[1:], BF)] * (blocks // 2), deps=(keep2,))
    got1 = high(blocks1)
    keep2, send2 = by_low(keep2, got2, (blocks1[0],))
    got2 = across("tensor", 2, send2)
    small = total((small, got3), F32)
    got3 = across("tensor", 2, small)
    own1 = rest(total((blocks1[0], *got1), BF, (keep2,)), BF)
    all1 = gather(own1)
    gx_own = settle(arr_gx, (own1,))
    gx4 = four(gx_own)
    blocks2 = call(joined_kernel, (keep2, got2), [shape(keep2.shape[1:], BF)] * (blocks // 2), deps=(gx_own,))
    got2 = high(blocks2)
    small = total((small, got3), F32, (blocks2[0],))
    small = total((small, *[across("dp", 2 * j, small) for j in range(1, blocks // 2)]), F32)
    own2 = rest(total((blocks2[0], *got2), BF, (gx_own,)), BF)
    all2 = gather(own2)
    small = rest(small, F32)
    layer_output = widen(y4)
    up_grad, down_grad, out_grad = call(
        functools.partial(spread_first_kernel, blocks), (ids, *all1),
        [shape((width, units), F32), shape((units, width), F32), shape((lanes, width), F32)], scalars=1,
    )
    qkv_grad = call(
        functools.partial(spread_second_kernel, blocks), (ids, *all2), [shape((3, width, lanes), F32)], scalars=1
    )[0]
    input_grad = widen(gx4)
    up_bias_grad = lax.dynamic_index_in_dim(small, tensor, 0, keepdims=False)
    qv_bias_grad = lax.dynamic_slice_in_dim(small[8:10], tensor * lanes, lanes, 1)
    return (
        layer_output,
        input_grad,
        qkv_grad,
        qv_bias_grad,
        out_grad,
        small[4],
        up_grad,
        up_bias_grad,
        down_grad,
        small[5],
        jnp.sum(small[6:8], axis=1),
    )


def solution(mesh):
    in_specs = (
        P(None, "dp", None), P(None, "dp", None), P(), P(None, "dp", None),
        P(None, None, "tensor"), P(None, "tensor"), P("tensor", None), P(),
        P(None, "tensor"), P("tensor"), P("tensor", None), P(), P(),
    )
    out_specs = (
        P(None, "dp", None), P(None, "dp", None), P(None, None, "tensor"), P(None, "tensor"),
        P("tensor", None), P(), P(None, "tensor"), P("tensor"), P("tensor", None), P(), P(),
    )
    return jax.shard_map(per_device, mesh=mesh, in_specs=in_specs, out_specs=out_specs, check_vma=False)
```

time: 1970 us -> 341 us (0.17)
  waiting for transfers between devices: 571 us -> 69.8 us
  other arithmetic: 436 us -> 2.09 us
  local copies, waits for them, and re-layouts: 362 us -> 17.7 us
  matrix products: 297 us -> 0 us
  Pallas kernels: 0 us -> 155 us
  blocking collectives: 128 us -> 0 us
  loops' own time: 69.1 us -> 0 us
    dot_general x128 -> x0, matrix products: 288 us -> none  [the longest x24 60.4 us: masked_scores(): jnp.einsum('qhe,khe->hqk', query_block, key_heads, preferred_element_type...]
    scatter-add x4 -> x0, other arithmetic: 228 us -> none  [per_device(): jnp.nonzero(owners == group_id, size=tok_rows)[0].astype(jnp.int32)]
    all_to_all x13 -> x4, waiting for transfers between devices: 213 us -> 5.81 us  [exchange(): lax.all_to_all(rows_out.reshape(groups, rows // groups, width), 'dp', 0,...]
    reduce_scatter x16 -> x0, waiting for transfers between devices: 184 us -> none  [the longest x4 74.2 us: per_device(): lax.psum_scatter(jnp.einsum('cse,cde->sd', grad_qkv, qkv_weight, preferre...]
    gather x36 -> x0, local copies, waits for them, and re-layouts: 174 us -> none  [the longest x4 29.4 us: per_device(): output_all[arrival_slots]]
    pallas_call x0 -> x25, Pallas kernels: none -> 155 us  [the longest x21 131 us: call(): pl.pallas_call(body, out_shape=list(outs), in_specs=[smem()] * scalars +...]
    all_to_all x3 -> x0, blocking collectives: 90.2 us -> none  [per_device(): lax.all_to_all(cotangent[micro_index][send_rows], 'dp', split_axis=0, con...]
    all_gather x24 -> x3, waiting for transfers between devices: 77 us -> 3.68 us  [the longest x1 3.64 us: per_device(): wd = lax.all_gather(down_weight, 'tensor', axis=0)]
  transfers between devices with their start and end apart: 55 -> 51, of which waited for: 21 -> 20; matrix products, arithmetic and copies ran while one was open for 47% -> 2% of each run, Pallas kernels for 0% -> 35%
where the time goes in v1:
time: 341 us; the launch traced here: 336 us
  Pallas kernels  155 us (45%)
  starting transfers between devices  77.2 us (23%)
  waiting for transfers between devices  69.8 us (20%)
  local copies, waits for them, and re-layouts  17.7 us (5%)
  between operations  14.4 us (4%)
    pallas_call x21, Pallas kernels, call(): pl.pallas_call(body, out_shape=list(outs), in_specs=[smem()] * scalars +...  131 us
    ppermute x44, waiting for transfers between devices, across(): return lax.ppermute(value, axis, [(i, i ^ bit) for i in range(count)])  58.2 us
    ppermute x44, starting transfers between devices, across(): return lax.ppermute(value, axis, [(i, i ^ bit) for i in range(count)])  55.6 us
    all_to_all x4, starting transfers between devices, exchange(): lax.all_to_all(rows_out.reshape(groups, rows // groups, width), 'dp', 0,...  21.5 us
    unnamed x112, local copies, waits for them, and re-layouts  13.8 us
    pallas_call x2, Pallas kernels, widen(): pl.pallas_call(widen_kernel, out_shape=shape((tensors, rows, width), F32)...  13.1 us
  transfers between devices with their start and end apart: 51, of which 20 were waited for; matrix products, arithmetic and copies ran while one was open for 2% of the time, Pallas kernels for 35%

profile of v1, /device:TPU:0, one launch (start us, length us, event | category | flops | bytes accessed | tf_op | source)
XLA Modules:
  0.0 336.1 jit_solution(1237864559589086164)
XLA Ops:
  9.3 6.1 %shard_map.212 = (bf16[1024,512]{1,0:T(8,128)(2,1)}, s32[8,128]{1,0:T(8,128)}, s32[1024,128]{1,0:T(8,128)}) custom-call(s32[2]{0:T(128)} %pad_add_fusion.ids_ref.refs_0_, s32[4,8192]{1,0:T(4,128)} %src_ref.3, bf16[4,1024,512]{2,1,0:T(8,128)(2,1)} %x_ref.1), custom_call_target="tpu_custom_call" | custom-call | flops 1073741824 | bytes 4194304 | tf_op jit(solution)/shard_map/pallas_call | solution.py:449
  15.5 7.4 %all-to-all-start.1 = ((bf16[8,128,512]{2,1,0:T(8,128)(2,1)}), bf16[8,128,512]{2,1,0:T(8,128)(2,1)S(1)}, u32[]{:S(2)}, u32[]{:S(2)}) async-start(bf16[8,128,512]{2,1,0:T(8,128)(2,1)} %bitcast.21), calls=%async_computation.1 | async-start | bytes 2097152 | tf_op jit(solution)/shard_map/all_to_all | solution.py:455
  25.3 7.1 %collective-permute-done.1.refs_8_ = bf16[128,512]{1,0:T(8,128)(2,1)S(1)} collective-permute-done((bf16[128,512]{1,0:T(8,128)(2,1)S(1)}, bf16[128,512]{1,0:T(8,128)(2,1)S(1)}, u32[]{:S(2)}, u32[]{:S(2)}) %collective-permute-start.1) | collective-permute-done | bytes 131104 | tf_op jit(solution)/shard_map/ppermute | solution.py:417
  36.1 4.9 %shard_map.213 = (bf16[1024,512]{1,0:T(8,128)(2,1)}, s32[8,1024]{1,0:T(8,128)}, s32[1024,128]{1,0:T(8,128)}) custom-call(s32[2]{0:T(128)} %pad_add_fusion.ids_ref.refs_0_, s32[4,8192]{1,0:T(4,128)} %src_ref.3, bf16[4,1024,512]{2,1,0:T(8,128)(2,1)} %g_ref.1, s32[8,128]{1,0:T(8,128)} %get-tuple-element.57.srow_ref), custom_call_target="tpu_custom_call" | custom-call | flops 1073741824 | bytes 4194304 | tf_op jit(solution)/shard_map/pallas_call | solution.py:458
  42.8 5.8 %all-to-all-done.1 = bf16[8,128,512]{2,1,0:T(8,128)(2,1)S(1)} async-done(((bf16[8,128,512]{2,1,0:T(8,128)(2,1)}), bf16[8,128,512]{2,1,0:T(8,128)(2,1)S(1)}, u32[]{:S(2)}, u32[]{:S(2)}) %all-to-all-start.1) | async-done | bytes 1048608 | tf_op jit(solution)/shard_map/all_to_all | solution.py:455
  48.6 3.8 %all-to-all-start = ((bf16[8,128,512]{2,1,0:T(8,128)(2,1)}), bf16[8,128,512]{2,1,0:T(8,128)(2,1)S(1)}, u32[]{:S(2)}, u32[]{:S(2)}) async-start(bf16[8,128,512]{2,1,0:T(8,128)(2,1)} %bitcast.23), calls=%async_computation | async-start | bytes 2097152 | tf_op jit(solution)/shard_map/all_to_all | solution.py:455
  53.2 26.3 %shard_map.214 = (bf16[1024,512]{1,0:T(8,128)(2,1)}, bf16[4,1024,128]{2,1,0:T(8,128)(2,1)}, bf16[4,1024,128]{2,1,0:T(8,128)(2,1)}, bf16[4,1024,128]{2,1,0:T(8,12...) custom-call(s32[2]{0:T(128)} %pad_add_fusion.ids_ref.refs_0_, ...), custom_call_target="tpu_custom_call" | custom-call | flops 27000000512 | bytes 16777216 | tf_op jit(solution)/shard_map/pallas_call | solution.py:390
  79.5 3.6 %all-gather.11.cloned.1.call-done = bf16[2048,512]{1,0:T(8,128)(2,1)} async-done(((bf16[512,512]{1,0:T(8,128)(2,1)}), bf16[2048,512]{1,0:T(8,128)(2,1)}) %all-gather.11.cloned.1.call-update) | async-done | bytes 2097168 | tf_op jit(solution)/shard_map/all_gather | solution.py:425
  83.2 30.5 %shard_map.215 = (bf16[1024,512]{1,0:T(8,128)(2,1)}, bf16[4,1024,128]{2,1,0:T(8,128)(2,1)}, f32[1024,512]{1,0:T(8,128)}, bf16[2,8,144,512]{3,2,1,0:T(8,128)(2,1)...) custom-call(s32[2]{0:T(128)} %pad_add_fusion.ids_ref.refs_0_, f32[2]{0:T(128)} %refs_1_.1, ...), custom_call_target="tpu_custom_call" | custom-call | flops 31000000512 | bytes 25165824 | tf_op jit(solution)/shard_map/pallas_call | solution.py:390
  114.0 5.5 %all-to-all-start.2 = ((bf16[8,128,512]{2,1,0:T(8,128)(2,1)}), bf16[8,128,512]{2,1,0:T(8,128)(2,1)S(1)}, u32[]{:S(2)}, u32[]{:S(2)}) async-start(bf16[8,128,512]{2,1,0:T(8,128)(2,1)} %bitcast.24), calls=%async_computation.2 | async-start | bytes 2097152 | tf_op jit(solution)/shard_map/all_to_all | solution.py:455
  119.5 13.7 %shard_map.216.refs_2_ = bf16[3,2,1024,128]{3,2,1,0:T(8,128)(2,1)} custom-call(s32[3]{0:T(128)} %dynamic-slice_reduce_fusion.refs_1_.refs_0_, bf16[4,1024,128]{2,1,0:T(8,128)(2,1)} %get-tuple-element.69.refs_1_, bf16[4,1024,128]{2,1,0:T(8,128)(2,1)} %get-tuple-element.70.refs_2_, bf16[4,1024,128]{2,1,0:T(8,128)(2,1)} %get-tuple-element.71.refs_3_, ...), custom_call_target="tpu_custom_call" | custom-call | flops 14000000000 | bytes 8388608 | tf_op jit(solution)/shard_map/pallas_call | solution.py:390
  134.6 4.3 %shard_map.217 = (bf16[2,4,144,512]{3,2,1,0:T(8,128)(2,1)}, bf16[2,4,144,512]{3,2,1,0:T(8,128)(2,1)}) custom-call(bf16[2,8,144,512]{3,2,1,0:T(8,128)(2,1)} %get-tuple-element.74.refs_6_.refs_0_, bf16[2,8,144,512]{3,2,1,0:T(8,128)(2,1)} %copy-done.4, bf16[3,2,1024,128]{3,2,1,0:T(8,128)(2,1)} %shard_map.216.refs_2_), custom_call_target="tpu_custom_call" | custom-call | flops 1000000 | bytes 4194304 | tf_op jit(solution)/shard_map/pallas_call | solution.py:390
  140.9 14.1 %shard_map.218.refs_2_.refs_3_ = bf16[3,2,1024,128]{3,2,1,0:T(8,128)(2,1)} custom-call(s32[3]{0:T(128)} %dynamic-slice_reduce_fusion.refs_1_.refs_0_, bf16[4,1024,128]{2,1,0:T(8,128)(2,1)} %get-tuple-element.69.refs_1_, bf16[4,1024,128]{2,1,0:T(8,128)(2,1)} %get-tuple-element.70.refs_2_, bf16[4,1024,128]{2,1,0:T(8,128)(2,1)} %get-tuple-element.71.refs_3_, ...), custom_call_target="tpu_custom_call" | custom-call | flops 14000000000 | bytes 8388608 | tf_op jit(solution)/shard_map/pallas_call | solution.py:390
  156.0 3.6 %shard_map.219.refs_0_.refs_8_ = bf16[1024,512]{1,0:T(8,128)(2,1)} custom-call(bf16[1024,512]{1,0:T(8,128)(2,1)} %bitcast.18, s32[1024,128]{1,0:T(8,128)} %get-tuple-element.68.refs_1_, bf16[3,2,1024,128]{3,2,1,0:T(8,128)(2,1)} %shard_map.218.refs_2_.refs_3_), custom_call_target="tpu_custom_call" | custom-call | flops 1000000000 | bytes 4194304 | tf_op jit(solution)/shard_map/pallas_call | solution.py:390
  159.6 10.1 %shard_map.221 = (bf16[1024,512]{1,0:T(8,128)(2,1)}, bf16[2,8,192,128]{3,2,1,0:T(8,128)(2,1)}, bf16[2,8,192,128]{3,2,1,0:T(8,128)(2,1)}, f32[16,512]{1,0:T(8,128)}) custom-call(s32[2]{0:T(128)} %pad_add_fusion.ids_ref.refs_0_, bf16[1024,512]{1,0:T(8,128)(2,1)} %get-tuple-element.77.refs_1_, bf16[3,2,1024,128]{3,2,1,0:T(8,128)(2,1)} %shard_map.216.refs_2_, ...), custom_call_target="tpu_custom_call" | custom-call | flops 7000000000 | bytes 8388608 | tf_op jit(solution)/shard_map/pallas_call | solution.py:390
  169.7 4.7 %all-to-all-start.3 = ((bf16[8,128,512]{2,1,0:T(8,128)(2,1)}), bf16[8,128,512]{2,1,0:T(8,128)(2,1)S(1)}, u32[]{:S(2)}, u32[]{:S(2)}) async-start(bf16[8,128,512]{2,1,0:T(8,128)(2,1)} %bitcast.17), calls=%async_computation.3 | async-start | bytes 2097152 | tf_op jit(solution)/shard_map/all_to_all | solution.py:455
  175.6 2.8 shard_map.222
  181.3 2.4 shard_map.223
  185.7 9.0 %collective-permute-done.11.refs_1_ = bf16[4,144,512]{2,1,0:T(8,128)(2,1)S(1)} collective-permute-done((bf16[4,144,512]{2,1,0:T(8,128)(2,1)}, bf16[4,144,512]{2,1,0:T(8,128)(2,1)S(1)}, u32[]{:S(2)}, u32[]{:S(2)}) %collective-permute-start.11) | collective-permute-done | bytes 589856 | tf_op jit(solution)/shard_map/ppermute | solution.py:417
  204.8 8.6 %collective-permute-done.14.refs_2_ = bf16[144,512]{1,0:T(8,128)(2,1)S(1)} collective-permute-done((bf16[144,512]{1,0:T(8,128)(2,1)}, bf16[144,512]{1,0:T(8,128)(2,1)S(1)}, u32[]{:S(2)}, u32[]{:S(2)}) %collective-permute-start.14) | collective-permute-done | bytes 147488 | tf_op jit(solution)/shard_map/ppermute | solution.py:417
  217.0 3.7 %shard_map.227.refs_0_.refs_2_.refs_4_ = bf16[1024,512]{1,0:T(8,128)(2,1)} custom-call(bf16[1024,512]{1,0:T(8,128)(2,1)} %bitcast.20, s32[1024,128]{1,0:T(8,128)} %get-tuple-element.68.refs_1_, bf16[144,512]{1,0:T(8,128)(2,1)} %shard_map.226.refs_2_.refs_1_), custom_call_target="tpu_custom_call" | custom-call | flops 1000000000 | bytes 4194304 | tf_op jit(solution)/shard_map/pallas_call | solution.py:390
  227.5 2.7 collective-permute-done.32.refs_1_
  233.6 13.1 %collective-permute-done.20.refs_1_ = bf16[4,192,128]{2,1,0:T(8,128)(2,1)S(1)} collective-permute-done((bf16[4,192,128]{2,1,0:T(8,128)(2,1)}, bf16[4,192,128]{2,1,0:T(8,128)(2,1)S(1)}, u32[]{:S(2)}, u32[]{:S(2)}) %collective-permute-start.20) | collective-permute-done | bytes 196640 | tf_op jit(solution)/shard_map/ppermute | solution.py:417
  253.4 3.6 %collective-permute-start.35 = (f32[16,512]{1,0:T(8,128)}, f32[16,512]{1,0:T(8,128)S(1)}, u32[]{:S(2)}, u32[]{:S(2)}) collective-permute-start(f32[16,512]{1,0:T(8,128)} %shard_map.234.refs_0_), channel_id=1, source_target_pairs={{0,16},{4,20},{8,24},{12,28},{16,0},{20,4},{24,8},{28,12},{1,17},{... | collective-permute-start | bytes 98312 | tf_op jit(solution)/shard_map/ppermute | solution.py:417
  259.5 2.6 collective-permute-start.34
  266.2 2.4 collective-permute-start.23
  272.9 4.8 %collective-permute-start.40 = (bf16[144,512]{1,0:T(8,128)(2,1)S(1)}, bf16[144,512]{1,0:T(8,128)(2,1)S(1)}, u32[]{:S(2)}, u32[]{:S(2)}) collective-permute-start(bf16[144,512]{1,0:T(8,128)(2,1)S(1)} %copy-done.14), channel_id=1, source_target_pairs={{0,16},{4,20},{8,24},{12,28},{16,0},{20,4},{24,8},{28,12},{1,17},{... | collective-permute-start | bytes 442376 | tf_op jit(solution)/shard_map/ppermute | solution.py:417
  277.7 4.3 %collective-permute-start.38 = (bf16[144,512]{1,0:T(8,128)(2,1)S(1)}, bf16[144,512]{1,0:T(8,128)(2,1)S(1)}, u32[]{:S(2)}, u32[]{:S(2)}) collective-permute-start(bf16[144,512]{1,0:T(8,128)(2,1)S(1)} %copy-done.14), channel_id=1, source_target_pairs={{0,8},{4,12},{8,0},{12,4},{16,24},{20,28},{24,16},{28,20},{1,9},{5... | collective-permute-start | bytes 442376 | tf_op jit(solution)/shard_map/ppermute | solution.py:417
  290.8 2.9 collective-permute-done.29.refs_7_
  309.0 6.5 %shard_map.220 = f32[4,1024,512]{2,1,0:T(8,128)} custom-call(s32[2]{0:T(128)} %pad_add_fusion.ids_ref.refs_0_, bf16[1024,512]{1,0:T(8,128)(2,1)} %shard_map.219.refs_0_.refs_8_, bf16[1024,512]{1,0:T(8,128)(2,1)} %collective-permute-done.7.refs_1_, bf16[1024,512]{1,0:T(8,128)(2,1)} %copy-done.6, bf16[1024,512]{1,0:T(8,128)(2,1)} %collective-permute-done.9.refs_3_), custom_call_target="tpu_custom_call" | custom-call | flops 1000000 | bytes 12582912 | tf_op jit(solution)/shard_map/pallas_call | solution.py:534
  318.9 2.9 shard_map.236
  322.8 6.6 %shard_map.228 = f32[4,1024,512]{2,1,0:T(8,128)} custom-call(s32[2]{0:T(128)} %pad_add_fusion.ids_ref.refs_0_, bf16[1024,512]{1,0:T(8,128)(2,1)} %shard_map.227.refs_0_.refs_2_.refs_4_, bf16[1024,512]{1,0:T(8,128)(2,1)} %copy-done.8, bf16[1024,512]{1,0:T(8,128)(2,1)} %copy-done.7, bf16[1024,512]{1,0:T(8,128)(2,1)} %collective-permute-done.19.refs_3_), custom_call_target="tpu_custom_call" | custom-call | flops 1000000 | bytes 12582912 | tf_op jit(solution)/shard_map/pallas_call | solution.py:534
  (220 shorter events, 91.3 us)
Async XLA Ops:
  7.2 45.4 %all-gather.7.cloned.1.call-start = ((), (), s32[]{:S(2)}) async-start(), calls=%async_computation.4 | async-start | bytes 1966080 | tf_op jit(solution)/shard_map/all_gather | solution.py:423
  7.9 71.6 %all-gather.9.cloned.1.call-start = ((), (), s32[]{:S(2)}) async-start(), calls=%async_computation.5 | async-start | bytes 2621440 | tf_op jit(solution)/shard_map/all_gather | solution.py:424
  15.5 33.2 %all-to-all-start.1 = ((bf16[8,128,512]{2,1,0:T(8,128)(2,1)}), bf16[8,128,512]{2,1,0:T(8,128)(2,1)S(1)}, u32[]{:S(2)}, u32[]{:S(2)}) async-start(bf16[8,128,512]{2,1,0:T(8,128)(2,1)} %bitcast.21), calls=%async_computation.1 | async-start | bytes 2097152 | tf_op jit(solution)/shard_map/all_to_all | solution.py:455
  22.9 60.3 %all-gather.11.cloned.1.call-start = ((), (), s32[]{:S(2)}) async-start(), calls=%async_computation.6 | async-start | bytes 2621440 | tf_op jit(solution)/shard_map/all_gather | solution.py:425
  23.6 8.7 %collective-permute-start.1 = (bf16[128,512]{1,0:T(8,128)(2,1)S(1)}, bf16[128,512]{1,0:T(8,128)(2,1)S(1)}, u32[]{:S(2)}, u32[]{:S(2)}) collective-permute-start(bf16[128,512]{1,0:T(8,128)(2,1)S(1)} %copy-done.49), channel_id=1, source_target_pairs={{0,2},{1,3},{2,0},{3,1},{4,6},{5,7},{6,4},{7,5},{8,10},{9,11},{10,... | collective-permute-start | bytes 393224 | tf_op jit(solution)/shard_map/ppermute | solution.py:417
  25.2 27.3 %collective-permute-start = (bf16[128,512]{1,0:T(8,128)(2,1)S(1)}, bf16[128,512]{1,0:T(8,128)(2,1)S(1)}, u32[]{:S(2)}, u32[]{:S(2)}) collective-permute-start(bf16[128,512]{1,0:T(8,128)(2,1)S(1)} %copy-done.49), channel_id=1, source_target_pairs={{0,1},{1,0},{2,3},{3,2},{4,5},{5,4},{6,7},{7,6},{8,9},{9,8},{10,11... | collective-permute-start | bytes 393224 | tf_op jit(solution)/shard_map/ppermute | solution.py:417
  32.4 20.2 %collective-permute-start.2 = (bf16[128,512]{1,0:T(8,128)(2,1)S(1)}, bf16[128,512]{1,0:T(8,128)(2,1)S(1)}, u32[]{:S(2)}, u32[]{:S(2)}) collective-permute-start(bf16[128,512]{1,0:T(8,128)(2,1)S(1)} %collective-permute-done.1.refs_8_), channel_id=1, source_target_pairs={{0,1},{1,0},{2,3},{3,2},{4,5},{5,4},{6,7},{7,6},{8,9},{9,8},{10,11... | collective-permute-start | bytes 393224 | tf_op jit(solution)/shard_map/ppermute | solution.py:417
  33.7 18.7 %collective-permute-start.3 = (bf16[8,128]{1,0:T(8,128)(2,1)S(1)}, bf16[8,128]{1,0:T(8,128)(2,1)S(1)}, u32[]{:S(2)}, u32[]{:S(2)}) collective-permute-start(bf16[8,128]{1,0:T(8,128)(2,1)S(1)} %maximum_maximum_fusion.refs_10_), channel_id=1, source_target_pairs={{0,1},{1,0},{2,3},{3,2},{4,5},{5,4},{6,7},{7,6},{8,9},{9,8},{10,11... | collective-permute-start | bytes 6152 | tf_op jit(solution)/shard_map/ppermute | solution.py:417
  36.1 16.4 %collective-permute-start.5 = (bf16[8,128]{1,0:T(8,128)(2,1)S(1)}, bf16[8,128]{1,0:T(8,128)(2,1)S(1)}, u32[]{:S(2)}, u32[]{:S(2)}) collective-permute-start(bf16[8,128]{1,0:T(8,128)(2,1)S(1)} %collective-permute-done.4.refs_12_), channel_id=1, source_target_pairs={{0,1},{1,0},{2,3},{3,2},{4,5},{5,4},{6,7},{7,6},{8,9},{9,8},{10,11... | collective-permute-start | bytes 6152 | tf_op jit(solution)/shard_map/ppermute | solution.py:417
  48.6 30.8 %all-to-all-start = ((bf16[8,128,512]{2,1,0:T(8,128)(2,1)}), bf16[8,128,512]{2,1,0:T(8,128)(2,1)S(1)}, u32[]{:S(2)}, u32[]{:S(2)}) async-start(bf16[8,128,512]{2,1,0:T(8,128)(2,1)} %bitcast.23), calls=%async_computation | async-start | bytes 2097152 | tf_op jit(solution)/shard_map/all_to_all | solution.py:455
  113.7 19.5 %collective-permute-start.6 = (bf16[2,8,144,512]{3,2,1,0:T(8,128)(2,1)}, bf16[2,8,144,512]{3,2,1,0:T(8,128)(2,1)S(1)}, u32[]{:S(2)}, u32[]{:S(2)}) collective-permute-start(bf16[2,8,144,512]{3,2,1,0:T(8,128)(2,1)} %get-tuple-element.75), channel_id=1, source_target_pairs={{0,1},{1,0},{2,3},{3,2},{4,5},{5,4},{6,7},{7,6},{8,9},{9,8},{10,11... | collective-permute-start | bytes 7077896 | tf_op jit(solution)/shard_map/ppermute | solution.py:417
  114.0 41.0 %all-to-all-start.2 = ((bf16[8,128,512]{2,1,0:T(8,128)(2,1)}), bf16[8,128,512]{2,1,0:T(8,128)(2,1)S(1)}, u32[]{:S(2)}, u32[]{:S(2)}) async-start(bf16[8,128,512]{2,1,0:T(8,128)(2,1)} %bitcast.24), calls=%async_computation.2 | async-start | bytes 2097152 | tf_op jit(solution)/shard_map/all_to_all | solution.py:455
  138.9 35.6 %collective-permute-start.10 = (bf16[2,4,144,512]{3,2,1,0:T(8,128)(2,1)}, bf16[2,4,144,512]{3,2,1,0:T(8,128)(2,1)S(1)}, u32[]{:S(2)}, u32[]{:S(2)}) collective-permute-start(bf16[2,4,144,512]{3,2,1,0:T(8,128)(2,1)} %get-tuple-element.82), channel_id=1, source_target_pairs={{0,4},{4,0},{8,12},{12,8},{16,20},{20,16},{24,28},{28,24},{1,5},{5... | collective-permute-start | bytes 3538952 | tf_op jit(solution)/shard_map/ppermute | solution.py:417
  169.7 46.3 %all-to-all-start.3 = ((bf16[8,128,512]{2,1,0:T(8,128)(2,1)}), bf16[8,128,512]{2,1,0:T(8,128)(2,1)S(1)}, u32[]{:S(2)}, u32[]{:S(2)}) async-start(bf16[8,128,512]{2,1,0:T(8,128)(2,1)} %bitcast.17), calls=%async_computation.3 | async-start | bytes 2097152 | tf_op jit(solution)/shard_map/all_to_all | solution.py:455
  178.3 16.3 %collective-permute-start.11 = (bf16[4,144,512]{2,1,0:T(8,128)(2,1)}, bf16[4,144,512]{2,1,0:T(8,128)(2,1)S(1)}, u32[]{:S(2)}, u32[]{:S(2)}) collective-permute-start(bf16[4,144,512]{2,1,0:T(8,128)(2,1)} %get-tuple-element.84), channel_id=1, source_target_pairs={{0,2},{1,3},{2,0},{3,1},{4,6},{5,7},{6,4},{7,5},{8,10},{9,11},{10,... | collective-permute-start | bytes 1769480 | tf_op jit(solution)/shard_map/ppermute | solution.py:417
  178.9 42.3 %collective-permute-start.8 = (bf16[1024,512]{1,0:T(8,128)(2,1)S(1)}, bf16[1024,512]{1,0:T(8,128)(2,1)S(1)}, u32[]{:S(2)}, u32[]{:S(2)}) collective-permute-start(bf16[1024,512]{1,0:T(8,128)(2,1)S(1)} %copy-done.2), channel_id=1, source_target_pairs={{0,2},{1,3},{2,0},{3,1},{4,6},{5,7},{6,4},{7,5},{8,10},{9,11},{10,... | collective-permute-start | bytes 3145736 | tf_op jit(solution)/shard_map/ppermute | solution.py:417
  183.7 18.3 %collective-permute-start.16 = (bf16[2,4,192,128]{3,2,1,0:T(8,128)(2,1)}, bf16[2,4,192,128]{3,2,1,0:T(8,128)(2,1)S(1)}, u32[]{:S(2)}, u32[]{:S(2)}) collective-permute-start(bf16[2,4,192,128]{3,2,1,0:T(8,128)(2,1)} %get-tuple-element.92), channel_id=1, source_target_pairs={{0,4},{4,0},{8,12},{12,8},{16,20},{20,16},{24,28},{28,24},{1,5},{5... | collective-permute-start | bytes 1179656 | tf_op jit(solution)/shard_map/ppermute | solution.py:417
  199.6 13.8 %collective-permute-start.14 = (bf16[144,512]{1,0:T(8,128)(2,1)}, bf16[144,512]{1,0:T(8,128)(2,1)S(1)}, u32[]{:S(2)}, u32[]{:S(2)}) collective-permute-start(bf16[144,512]{1,0:T(8,128)(2,1)} %get-tuple-element.90), channel_id=1, source_target_pairs={{0,16},{4,20},{8,24},{12,28},{16,0},{20,4},{24,8},{28,12},{1,17},{... | collective-permute-start | bytes 442376 | tf_op jit(solution)/shard_map/ppermute | solution.py:417
  202.0 11.5 %collective-permute-start.15 = (bf16[144,512]{1,0:T(8,128)(2,1)}, bf16[144,512]{1,0:T(8,128)(2,1)S(1)}, u32[]{:S(2)}, u32[]{:S(2)}) collective-permute-start(bf16[144,512]{1,0:T(8,128)(2,1)} %get-tuple-element.91), channel_id=1, source_target_pairs={{0,24},{4,28},{8,16},{12,20},{16,8},{20,12},{24,0},{28,4},{1,25},{... | collective-permute-start | bytes 442376 | tf_op jit(solution)/shard_map/ppermute | solution.py:417
  202.0 55.0 %collective-permute-start.7 = (bf16[1024,512]{1,0:T(8,128)(2,1)S(1)}, bf16[1024,512]{1,0:T(8,128)(2,1)}, u32[]{:S(2)}, u32[]{:S(2)}) collective-permute-start(bf16[1024,512]{1,0:T(8,128)(2,1)S(1)} %copy-done.2), channel_id=1, source_target_pairs={{0,1},{1,0},{2,3},{3,2},{4,5},{5,4},{6,7},{7,6},{8,9},{9,8},{10,11... | collective-permute-start | bytes 3145736 | tf_op jit(solution)/shard_map/ppermute | solution.py:417
  220.7 36.5 %collective-permute-start.18 = (bf16[1024,512]{1,0:T(8,128)(2,1)}, bf16[1024,512]{1,0:T(8,128)(2,1)S(1)}, u32[]{:S(2)}, u32[]{:S(2)}) collective-permute-start(bf16[1024,512]{1,0:T(8,128)(2,1)} %shard_map.227.refs_0_.refs_2_.refs_4_), channel_id=1, source_target_pairs={{0,2},{1,3},{2,0},{3,1},{4,6},{5,7},{6,4},{7,5},{8,10},{9,11},{10,... | collective-permute-start | bytes 3145736 | tf_op jit(solution)/shard_map/ppermute | solution.py:417
  221.2 80.1 %collective-permute-start.9 = (bf16[1024,512]{1,0:T(8,128)(2,1)S(1)}, bf16[1024,512]{1,0:T(8,128)(2,1)}, u32[]{:S(2)}, u32[]{:S(2)}) collective-permute-start(bf16[1024,512]{1,0:T(8,128)(2,1)S(1)} %collective-permute-done.8.refs_2_), channel_id=1, source_target_pairs={{0,1},{1,0},{2,3},{3,2},{4,5},{5,4},{6,7},{7,6},{8,9},{9,8},{10,11... | collective-permute-start | bytes 3145736 | tf_op jit(solution)/shard_map/ppermute | solution.py:417
  221.2 25.4 %collective-permute-start.20 = (bf16[4,192,128]{2,1,0:T(8,128)(2,1)}, bf16[4,192,128]{2,1,0:T(8,128)(2,1)S(1)}, u32[]{:S(2)}, u32[]{:S(2)}) collective-permute-start(bf16[4,192,128]{2,1,0:T(8,128)(2,1)} %get-tuple-element.94), channel_id=1, source_target_pairs={{0,2},{1,3},{2,0},{3,1},{4,6},{5,7},{6,4},{7,5},{8,10},{9,11},{10,... | collective-permute-start | bytes 589832 | tf_op jit(solution)/shard_map/ppermute | solution.py:417
  232.1 16.9 %collective-permute-start.33 = (f32[16,512]{1,0:T(8,128)}, f32[16,512]{1,0:T(8,128)S(1)}, u32[]{:S(2)}, u32[]{:S(2)}) collective-permute-start(f32[16,512]{1,0:T(8,128)} %shard_map.233.refs_0_), channel_id=1, source_target_pairs={{0,2},{1,3},{2,0},{3,1},{4,6},{5,7},{6,4},{7,5},{8,10},{9,11},{10,... | collective-permute-start | bytes 98312 | tf_op jit(solution)/shard_map/ppermute | solution.py:417
  257.0 9.2 %collective-permute-start.21 = (bf16[192,128]{1,0:T(8,128)(2,1)}, bf16[192,128]{1,0:T(8,128)(2,1)S(1)}, u32[]{:S(2)}, u32[]{:S(2)}) collective-permute-start(bf16[192,128]{1,0:T(8,128)(2,1)} %get-tuple-element.96), channel_id=1, source_target_pairs={{0,8},{4,12},{8,0},{12,4},{16,24},{20,28},{24,16},{28,20},{1,9},{5... | collective-permute-start | bytes 147464 | tf_op jit(solution)/shard_map/ppermute | solution.py:417
  257.1 64.6 %collective-permute-start.17 = (bf16[1024,512]{1,0:T(8,128)(2,1)}, bf16[1024,512]{1,0:T(8,128)(2,1)S(1)}, u32[]{:S(2)}, u32[]{:S(2)}) collective-permute-start(bf16[1024,512]{1,0:T(8,128)(2,1)} %shard_map.227.refs_0_.refs_2_.refs_4_), channel_id=1, source_target_pairs={{0,1},{1,0},{2,3},{3,2},{4,5},{5,4},{6,7},{7,6},{8,9},{9,8},{10,11... | collective-permute-start | bytes 3145736 | tf_op jit(solution)/shard_map/ppermute | solution.py:417
  257.2 64.6 %collective-permute-start.19 = (bf16[1024,512]{1,0:T(8,128)(2,1)S(1)}, bf16[1024,512]{1,0:T(8,128)(2,1)}, u32[]{:S(2)}, u32[]{:S(2)}) collective-permute-start(bf16[1024,512]{1,0:T(8,128)(2,1)S(1)} %collective-permute-done.18.refs_2_), channel_id=1, source_target_pairs={{0,1},{1,0},{2,3},{3,2},{4,5},{5,4},{6,7},{7,6},{8,9},{9,8},{10,11... | collective-permute-start | bytes 3145736 | tf_op jit(solution)/shard_map/ppermute | solution.py:417
  272.9 11.0 %collective-permute-start.40 = (bf16[144,512]{1,0:T(8,128)(2,1)S(1)}, bf16[144,512]{1,0:T(8,128)(2,1)S(1)}, u32[]{:S(2)}, u32[]{:S(2)}) collective-permute-start(bf16[144,512]{1,0:T(8,128)(2,1)S(1)} %copy-done.14), channel_id=1, source_target_pairs={{0,16},{4,20},{8,24},{12,28},{16,0},{20,4},{24,8},{28,12},{1,17},{... | collective-permute-start | bytes 442376 | tf_op jit(solution)/shard_map/ppermute | solution.py:417
  277.7 9.9 %collective-permute-start.38 = (bf16[144,512]{1,0:T(8,128)(2,1)S(1)}, bf16[144,512]{1,0:T(8,128)(2,1)S(1)}, u32[]{:S(2)}, u32[]{:S(2)}) collective-permute-start(bf16[144,512]{1,0:T(8,128)(2,1)S(1)} %copy-done.14), channel_id=1, source_target_pairs={{0,8},{4,12},{8,0},{12,4},{16,24},{20,28},{24,16},{28,20},{1,9},{5... | collective-permute-start | bytes 442376 | tf_op jit(solution)/shard_map/ppermute | solution.py:417
  303.2 14.2 %collective-permute-start.43 = (bf16[144,512]{1,0:T(8,128)(2,1)}, bf16[144,512]{1,0:T(8,128)(2,1)S(1)}, u32[]{:S(2)}, u32[]{:S(2)}) collective-permute-start(bf16[144,512]{1,0:T(8,128)(2,1)} %copy-done.20), channel_id=1, source_target_pairs={{0,4},{4,0},{8,12},{12,8},{16,20},{20,16},{24,28},{28,24},{1,5},{5... | collective-permute-start | bytes 442376 | tf_op jit(solution)/shard_map/ppermute | solution.py:417
  304.8 12.6 %collective-permute-start.41 = (bf16[144,512]{1,0:T(8,128)(2,1)}, bf16[144,512]{1,0:T(8,128)(2,1)S(1)}, u32[]{:S(2)}, u32[]{:S(2)}) collective-permute-start(bf16[144,512]{1,0:T(8,128)(2,1)} %copy-done.21), channel_id=1, source_target_pairs={{0,4},{4,0},{8,12},{12,8},{16,20},{20,16},{24,28},{28,24},{1,5},{5... | collective-permute-start | bytes 442376 | tf_op jit(solution)/shard_map/ppermute | solution.py:417
  306.0 11.5 %collective-permute-start.39 = (bf16[144,512]{1,0:T(8,128)(2,1)}, bf16[144,512]{1,0:T(8,128)(2,1)S(1)}, u32[]{:S(2)}, u32[]{:S(2)}) collective-permute-start(bf16[144,512]{1,0:T(8,128)(2,1)} %copy-done.22), channel_id=1, source_target_pairs={{0,4},{4,0},{8,12},{12,8},{16,20},{20,16},{24,28},{28,24},{1,5},{5... | collective-permute-start | bytes 442376 | tf_op jit(solution)/shard_map/ppermute | solution.py:417
  (75 other events, 735.8 us)
Sparse Core Ops, SparseCore 0:
  9.6 25.1 all-gather.6
  36.3 22.5 all-gather.8
  60.5 22.5 all-gather.10
